TPU v7x, 512 devices: a whole 4x4x16 slice. The times are simulated.
512 devices in a mesh: ctx: 8 (over y, core), exp: 16 (over z), tp: 4 (over x).
Axes of the slice: x: 4, y: 4, z: 16, core: 2. Of those that a mesh axis runs over, the one named last changes fastest.
Arguments:
- mixer_input: bfloat16 [1024, 8192], P('ctx', ('exp', 'tp')), may hold values from -6 to 6
- step_sizes: float32 [1024, 8192], P('ctx', ('exp', 'tp')), may hold values from 0.015 to 0.5
- decay_rates: float32 [16, 8192], P(None, ('exp', 'tp')), as said below
- input_proj: float32 [16, 1024], P(None, 'ctx'), may hold values from -3 to 3
- output_proj: float32 [16, 1024], P(None, 'ctx'), may hold values from -1.5 to 1.5
- skip_gain: float32 [8192], P(('exp', 'tp')), may hold values from 0.5 to 1.5
- doc_starts: int32 [1024], P('ctx'), may hold values from 0 to 1, as said below
- ssm_grad: bfloat16 [1024, 8192], P('ctx', ('exp', 'tp')), may hold values from -6 to 6
- mixer_in_weight: bfloat16 [8192, 4096], P(('exp', 'tp'), 'ctx'), may hold values from -0.0078125 to 0.0078125
- residual_grad: bfloat16 [1024, 4096], P(('ctx', 'exp')), may hold values from -0.59765625 to 0.59765625
- expert_index_pairs: int32 [1024, 2], P(('ctx', 'exp')), may hold values from 0 to 15, all different within a row; in each aligned block of 8 rows (0 to 7, 8 to 15, ...) at most 3 rows name the same one
- route_probs: float32 [1024, 2], P(('ctx', 'exp')), may hold values from 0.05 to 0.6
- hidden_saved: bfloat16 [16, 7168, 384], P('exp', ('ctx', 'tp')), may hold values from -3 to 3
- down_weight: bfloat16 [16, 7168, 4096], P('exp', ('ctx', 'tp')), may hold values from -0.0625 to 0.0625
Outputs:
- ssm_input_grad: bfloat16 [1024, 8192], P('ctx', ('exp', 'tp'))
- step_grad: float32 [1024, 8192], P('ctx', ('exp', 'tp'))
- input_proj_grad: float32 [16, 1024], P(None, 'ctx')
- output_proj_grad: float32 [16, 1024], P(None, 'ctx')
- decay_grad: float32 [16, 8192], P(None, ('exp', 'tp'))
- skip_grad: float32 [8192], P(('exp', 'tp'))
- slot_hidden_gradient: bfloat16 [16, 7168, 384], P('exp', ('ctx', 'tp'))
- down_grad: bfloat16 [16, 7168, 4096], P('exp', ('ctx', 'tp'))
- prob_grad: float32 [1024, 2], P(('ctx', 'exp'))
Inputs may be any that keep to these rules, and one draw needn't show every extreme that they name: `expert_index_pairs`: in the rows of one device (each aligned block of 8 rows) no expert is named by more than 3 rows; the two experts of a row differ. `doc_starts`: 1 marks the first token of a document: the first token of the window and exactly one more token in each half of the window. `decay_rates`: negative.
All inputs are finite; a program needn't handle non-finite values.
Results may differ from a plain program's by a relative error of at most 0.033.
Values may be sent and summed in bfloat16 or wider, within the bound.
A program may use at most 64 MiB of HBM per device.

v0:
```python
import jax
import jax.numpy as jnp
from jax import lax
from jax.sharding import PartitionSpec as P


def from_behind(shard, axis, by):
    peers = lax.axis_size(axis)
    pairs = [(i, i + by) for i in range(peers) if 0 <= i + by < peers]
    return lax.ppermute(shard, axis, pairs)


def forward_blocks(start_state, log_decay, inflow, start_count):
    block_len = log_decay.shape[1]
    below_mask = jnp.arange(block_len)[:, None] >= jnp.arange(block_len)[None, :]

    def advance_block(carry_state, block_item):
        block_logs, block_in, block_marks = block_item
        totals = jnp.cumsum(block_logs, axis=0)
        joined = below_mask & (block_marks[:, None] == block_marks[None, :])
        spread = jnp.where(joined[:, :, None, None], totals[:, None] - totals[None, :], -jnp.inf)
        block_states = jnp.sum(jnp.exp(spread) * block_in[None], axis=1)
        carried = jnp.where((block_marks == 0)[:, None, None], jnp.exp(totals), 0.0)
        block_states = block_states + carried * carry_state[None]
        return (block_states[-1], block_states)

    return lax.scan(advance_block, start_state, (log_decay, inflow, start_count))


def backward_blocks(start_state, log_decay, source, start_count):
    block_len = log_decay.shape[1]
    above_mask = jnp.arange(block_len)[:, None] <= jnp.arange(block_len)[None, :]

    def retreat_block(incoming, block_item):
        block_logs, block_src, block_marks = block_item
        totals = jnp.cumsum(block_logs, axis=0)
        joined = above_mask & (block_marks[:, None] == block_marks[None, :])
        spread = jnp.where(joined[:, :, None, None], totals[None, :] - totals[:, None], -jnp.inf)
        adjoint = jnp.sum(jnp.exp(spread) * block_src[None], axis=1)
        trailing_damping = jnp.where(
            (block_marks == block_marks[-1])[:, None, None], jnp.exp(totals[-1][None] - totals), 0.0
        )
        adjoint = adjoint + trailing_damping * incoming[None]
        leaving = jnp.where(block_marks[0] == 0, jnp.exp(block_logs[0]), 0.0) * adjoint[0]
        return (leaving, adjoint)

    return lax.scan(retreat_block, start_state, (log_decay, source, start_count), reverse=True)


def shards(
    mixer_input,
    step_sizes,
    decay_rates,
    input_proj,
    output_proj,
    skip_gain,
    doc_starts,
    ssm_grad,
    mixer_in_weight,
    residual_grad,
    expert_index_pairs,
    route_probs,
    hidden_saved,
    down_weight,
):
    tokens, channels = step_sizes.shape
    state_count = decay_rates.shape[0]
    block_len = 16
    blocks = tokens // block_len
    inputs = mixer_input.astype(jnp.float32)
    grad_vals = ssm_grad.astype(jnp.float32)
    in_weights = input_proj.T[:, :, None]
    log_decay = (step_sizes[:, None, :] * decay_rates[None]).reshape(
        blocks, block_len, state_count, channels
    )
    keep_mask = (1 - doc_starts).astype(jnp.float32)
    decay_vals = (
        jnp.exp(log_decay.reshape(tokens, state_count, channels)) * keep_mask[:, None, None]
    )
    start_count = jnp.cumsum(doc_starts.reshape(blocks, block_len), axis=1)
    inflow = ((step_sizes * inputs)[:, None, :] * in_weights).reshape(
        blocks, block_len, state_count, channels
    )
    source = (grad_vals[:, None, :] * output_proj.T[:, :, None]).reshape(
        blocks, block_len, state_count, channels
    )
    device_decay = jnp.exp(jnp.sum(log_decay, axis=(0, 1))) * jnp.where(
        jnp.sum(doc_starts) == 0, 1.0, 0.0
    )
    zero_state = jnp.zeros((state_count, channels), jnp.float32)
    local_end, _ = forward_blocks(zero_state, log_decay, inflow, start_count)
    local_first, _ = backward_blocks(zero_state, log_decay, source, start_count)

    def pass_up(index_turn, carried):
        return from_behind(device_decay * carried + local_end, "ctx", 1)

    def pass_down(index_turn, carried):
        return from_behind(device_decay * carried + local_first, "ctx", -1)

    entering = lax.fori_loop(0, lax.axis_size("ctx") - 1, pass_up, zero_state)
    arriving = lax.fori_loop(0, lax.axis_size("ctx") - 1, pass_down, zero_state)
    _, history = forward_blocks(entering, log_decay, inflow, start_count)
    _, adjoint = backward_blocks(arriving, log_decay, source, start_count)
    history = history.reshape(tokens, state_count, channels)
    adjoint = adjoint.reshape(tokens, state_count, channels)
    previous = jnp.concatenate([entering[None], history[:-1]], axis=0)
    ssm_input_grad = (
        skip_gain * grad_vals + step_sizes * jnp.sum(adjoint * in_weights, axis=1)
    ).astype(jnp.bfloat16)
    step_grad = jnp.sum(
        adjoint * (decay_rates[None] * decay_vals * previous + inputs[:, None, :] * in_weights),
        axis=1,
    )
    in_part = jnp.sum(adjoint * (step_sizes * inputs)[:, None, :], axis=2).T
    out_part = jnp.sum(grad_vals[:, None, :] * history, axis=2).T
    decay_part = jnp.sum(adjoint * step_sizes[:, None, :] * decay_vals * previous, axis=0)
    skip_part = jnp.sum(grad_vals * inputs, axis=0)
    input_proj_grad, output_proj_grad = lax.psum((in_part, out_part), ("exp", "tp"))
    decay_grad, skip_grad = lax.psum((decay_part, skip_part), "ctx")
    token_part = jnp.dot(
        ssm_input_grad,
        lax.all_gather(mixer_in_weight, "ctx", axis=1, tiled=True),
        preferred_element_type=jnp.float32,
    )
    token_rows = lax.psum_scatter(
        token_part.astype(jnp.bfloat16), "exp", scatter_dimension=0, tiled=True
    )
    token_sum = lax.psum(token_rows, "tp").astype(jnp.float32)
    moe_grad = (token_sum + residual_grad.astype(jnp.float32)).astype(jnp.bfloat16)
    token_count, feature_count = moe_grad.shape
    groups = lax.axis_size("exp")
    ctx_count = lax.axis_size("ctx")
    weight = down_weight[0]
    hidden = hidden_saved[0]
    slot_count = hidden.shape[1]
    capacity = slot_count // (ctx_count * groups)
    chosen = expert_index_pairs.reshape(-1)
    onehot = (chosen[:, None] == jnp.arange(groups, dtype=jnp.int32)[None, :]).astype(jnp.int32)
    earlier = jnp.cumsum(onehot, axis=0) - onehot
    target = chosen * capacity + jnp.sum(earlier * onehot, axis=1)
    dispatch = jnp.arange(groups * capacity, dtype=jnp.int32)[:, None] == target[None, :]
    token_pick = jnp.sum(
        dispatch.reshape(groups * capacity, token_count, 2).astype(jnp.int32), axis=2
    ).astype(jnp.bfloat16)
    send_rows = (
        jnp.dot(token_pick, moe_grad, preferred_element_type=jnp.float32)
        .astype(jnp.bfloat16)
        .reshape(groups, capacity, feature_count)
    )
    send_probs = (
        jnp.sum(jnp.where(dispatch, route_probs.reshape(-1)[None, :], 0.0), axis=1)
        .astype(jnp.bfloat16)
        .reshape(groups, capacity)
    )
    wide_rows = jnp.broadcast_to(
        send_rows[None], (ctx_count, groups, capacity, feature_count)
    ).reshape(ctx_count * groups, capacity, feature_count)
    wide_probs = jnp.broadcast_to(send_probs[None], (ctx_count, groups, capacity)).reshape(
        ctx_count * groups, capacity
    )
    arrived_rows, arrived_probs = (
        lax.all_to_all(wide_rows, ("ctx", "exp"), split_axis=0, concat_axis=0, tiled=True),
        lax.all_to_all(wide_probs, ("ctx", "exp"), split_axis=0, concat_axis=0, tiled=True),
    )
    arrived_rows = arrived_rows.reshape(slot_count, feature_count)
    arrived_probs = arrived_probs.reshape(slot_count)
    direct = lax.dot_general(
        weight, arrived_rows, (((1,), (1,)), ((), ())), preferred_element_type=jnp.float32
    )
    slot_hidden_gradient = (direct * arrived_probs.astype(jnp.float32)[None, :]).astype(
        jnp.bfloat16
    )[None]
    totals_part = jnp.sum(hidden.astype(jnp.float32) * direct, axis=0)
    scaled = arrived_rows * arrived_probs[:, None]
    down_grad = jnp.dot(hidden, scaled, preferred_element_type=jnp.float32).astype(jnp.bfloat16)[
        None
    ]
    totals = lax.psum(totals_part, ("ctx", "tp"))
    own_totals = lax.dynamic_slice_in_dim(
        totals.reshape(ctx_count * groups, capacity), lax.axis_index("ctx") * groups, groups, 0
    )
    returned = lax.all_to_all(own_totals, "exp", split_axis=0, concat_axis=0, tiled=True)
    prob_grad = jnp.sum(jnp.where(dispatch, returned.reshape(-1)[:, None], 0.0), axis=0).reshape(
        token_count, 2
    )
    return (
        ssm_input_grad,
        step_grad,
        input_proj_grad,
        output_proj_grad,
        decay_grad,
        skip_grad,
        slot_hidden_gradient,
        down_grad,
        prob_grad,
    )


def solution(mesh):
    return jax.shard_map(
        shards,
        mesh=mesh,
        in_specs=(
            P("ctx", ("exp", "tp")),
            P("ctx", ("exp", "tp")),
            P(None, ("exp", "tp")),
            P(None, "ctx"),
            P(None, "ctx"),
            P(("exp", "tp")),
            P("ctx"),
            P("ctx", ("exp", "tp")),
            P(("exp", "tp"), "ctx"),
            P(("ctx", "exp"), None),
            P(("ctx", "exp"), None),
            P(("ctx", "exp"), None),
            P("exp", ("ctx", "tp"), None),
            P("exp", ("ctx", "tp"), None),
        ),
        out_specs=(
            P("ctx", ("exp", "tp")),
            P("ctx", ("exp", "tp")),
            P(None, "ctx"),
            P(None, "ctx"),
            P(None, ("exp", "tp")),
            P(("exp", "tp")),
            P("exp", ("ctx", "tp"), None),
            P("exp", ("ctx", "tp"), None),
            P(("ctx", "exp"), None),
        ),
        check_vma=False,
    )
```

profile of v0, /device:TPU:24, one launch (start us, length us, event | category | flops | bytes accessed | tf_op | source)
XLA Modules:
  0.0 1032.6 jit_solution(11301472444736718690)
XLA Ops:
  14.7 24.2 %while.79 = (s32[]{:T(128)}, f32[16,128]{1,0:T(8,128)S(1)}, s32[8,16]{1,0:T(8,128)S(1)}, f32[8,16,16,128]{3,2,1,0:T(8,128)S(1)}, f32[8,16,16,128]{3,2,1,0:T(8,128)}, /*index=5*/s32[]{:T(128)}) while((s32[]{:T(128)}, f32[16,128]{1,0:T(8,128)S(1)}, s32[8,16]{1,0:T(8,128)S(1)}, f32[8,16,16,128]{3,2,1,0:T(8,128)S(1)}, ...), condition=%wide.region_17.18_spmd.clone, body=%wide.region_14.17_spmd.clone.sunk | while | flops 2562834 | bytes 967468 | solution.py:27
  38.9 34.8 %while.77 = (s32[]{:T(128)}, f32[16,128]{1,0:T(8,128)S(1)}, f32[16,128]{1,0:T(8,128)S(1)}, f32[16,128]{1,0:T(8,128)S(1)}, s32[]{:T(128)}) while((s32[]{:T(128)}, f32[16,128]{1,0:T(8,128)S(1)}, f32[16,128]{1,0:T(8,128)S(1)}, f32[16,128]{1,0:T(8,128)S(1)}, s32[]{:T(128)}) %tuple.165), condition=%wide.region_19.20_spmd, body=%wide.region_18.19_spmd.sunk | while | flops 4098 | bytes 65637 | solution.py:100
  40.9 3.0 collective-permute-done.1
  45.8 3.0 collective-permute-done.1
  55.8 3.0 collective-permute-done.1
  60.7 3.0 collective-permute-done.1
  65.7 3.0 collective-permute-done.1
  74.8 30.2 %while.80 = (s32[]{:T(128)}, f32[16,128]{1,0:T(8,128)S(1)}, f32[8,16,16,128]{3,2,1,0:T(8,128)}, s32[8,16]{1,0:T(8,128)S(1)}, f32[8,16,16,128]{3,2,1,0:T(8,128)S(1)}, /*index=5*/f32[8,16,16,128]{3,2,1,0:T(8,128)}, s32[]{:T(128)}) while((s32[]{:T(128)}, f32[16,128]{1,0:T(8,128)S(1)}, f32[8,16,16,128]{3,2,1,0:T(8,128)}, ...), condition=%wide.region_23.24_spmd.clone, body=%wide.region_20.23_spmd.clone.sunk | while | flops 2661138 | bytes 1499976 | solution.py:27
  107.7 30.1 %while.81 = (s32[]{:T(128)}, f32[16,128]{1,0:T(8,128)S(1)}, s32[8,16]{1,0:T(8,128)S(1)}, f32[8,16,16,128]{3,2,1,0:T(8,128)S(1)}, f32[8,16,16,128]{3,2,1,0:T(8,12...) while((s32[]{:T(128)}, f32[16,128]{1,0:T(8,128)S(1)}, s32[8,16]{1,0:T(8,128)S(1)}, ...), condition=%wide.region_6.7_spmd.clone, body=%wide.region_3.6_spmd.clone.sunk | while | flops 2571029 | bytes 1000514 | solution.py:47
  137.7 33.1 %while.76 = (s32[]{:T(128)}, f32[16,128]{1,0:T(8,128)S(1)}, f32[16,128]{1,0:T(8,128)S(1)}, f32[16,128]{1,0:T(8,128)S(1)}, s32[]{:T(128)}) while((s32[]{:T(128)}, f32[16,128]{1,0:T(8,128)S(1)}, f32[16,128]{1,0:T(8,128)S(1)}, f32[16,128]{1,0:T(8,128)S(1)}, s32[]{:T(128)}) %tuple.191), condition=%wide.region_8.9_spmd, body=%wide.region_7.8_spmd.sunk | while | flops 4098 | bytes 65637 | solution.py:101
  141.0 3.6 collective-permute-start
  146.0 3.6 collective-permute-start
  151.0 3.6 collective-permute-start
  155.9 3.6 collective-permute-start
  160.9 3.6 collective-permute-start
  165.9 3.6 collective-permute-start
  171.9 36.0 %while.78 = (s32[]{:T(128)}, f32[16,128]{1,0:T(8,128)S(1)}, f32[8,16,16,128]{3,2,1,0:T(8,128)}, s32[8,16]{1,0:T(8,128)S(1)}, f32[8,16,16,128]{3,2,1,0:T(8,128)S(...) while((s32[]{:T(128)}, f32[16,128]{1,0:T(8,128)S(1)}, ...), condition=%wide.region_12.13_spmd.clone, body=%wide.region_9.12_spmd.clone.sunk | while | flops 2700052 | bytes 1410124 | solution.py:47
  214.9 75.1 %reduce-scatter.2.cloned.1.call-done = bf16[8,4096]{1,0:T(8,128)(2,1)} async-done(((bf16[128,4096]{1,0:T(8,128)(2,1)}), bf16[8,4096]{1,0:T(8,128)(2,1)}) %reduce-scatter.2.cloned.1.call-update) | async-done | bytes 65552 | tf_op jit(solution)/shard_map/reduce_scatter | solution.py:125
  290.1 56.3 %all-reduce.4.cloned.1.call-done = bf16[8,4096]{1,0:T(8,128)(2,1)} async-done(((bf16[8,4096]{1,0:T(8,128)(2,1)}), bf16[8,4096]{1,0:T(8,128)(2,1)}) %all-reduce.4.cloned.1.call-update) | async-done | bytes 65552 | tf_op jit(solution)/shard_map/psum | solution.py:128
  347.8 4.1 broadcast_in_dim.264
  351.8 17.5 %all-to-all-start = ((bf16[128,3,4096]{2,1,0:T(4,128)(2,1)}), bf16[128,3,4096]{2,1,0:T(4,128)(2,1)}, u32[]{:S(2)}, u32[]{:S(2)}) async-start(bf16[128,3,4096]{2,1,0:T(4,128)(2,1)} %bitcast.205), calls=%async_computation.1 | async-start | bytes 8388608 | tf_op jit(solution)/shard_map/all_to_all | solution.py:162
  369.3 185.4 %all-to-all-done = bf16[128,3,4096]{2,1,0:T(4,128)(2,1)} async-done(((bf16[128,3,4096]{2,1,0:T(4,128)(2,1)}), bf16[128,3,4096]{2,1,0:T(4,128)(2,1)}, u32[]{:S(2)}, u32[]{:S(2)}) %all-to-all-start) | async-done | bytes 3145760 | tf_op jit(solution)/shard_map/all_to_all | solution.py:162
  554.7 7.4 reshape.415
  562.1 3.1 multiply_reduce_fusion.10
  565.4 111.1 %psum.47 = f32[128,3]{1,0:T(8,128)S(1)} all-reduce(f32[128,3]{1,0:T(8,128)S(1)} %reshape.416), channel_id=1, replica_groups=mesh['ctx'=8,'exp'=16,'tp'=4] {'ctx','tp'}, use_global_device_ids=true, to_apply=%region_40.41 | all-reduce | flops 384 | bytes 3072 | tf_op jit(solution)/shard_map/psum | solution.py:178
  677.2 9.5 all-to-all-start.2
  686.6 23.1 %all-reduce.1 = (f32[16,128]{1,0:T(8,128)}, f32[128]{0:T(128)}) all-reduce(f32[16,128]{1,0:T(8,128)S(1)} %get-tuple-element.496, f32[128]{0:T(128)S(1)} %get-tuple-element.580), channel_id=1, replica_groups=mesh['ctx'=8,'exp'=16,'tp'=4] {'ctx'}, use_global_device_ids=true, to_apply=%region_30.31 | all-reduce | flops 2176 | bytes 17408 | tf_op jit(solution)/shard_map/psum | solution.py:119
  712.6 18.1 %all-to-all-start.1 = ((bf16[128,1,3]{2,1,0:T(2,128)(2,1)}), bf16[128,1,3]{2,1,0:T(2,128)(2,1)S(1)}, u32[]{:S(2)}, u32[]{:S(2)}) async-start(bf16[128,1,3]{2,1,0:T(2,128)(2,1)} %copy.71), calls=%async_computation.2 | async-start | bytes 131072 | tf_op jit(solution)/shard_map/all_to_all | solution.py:163
  730.7 275.6 %all-reduce = (f32[16,128]{1,0:T(8,128)}, f32[16,128]{1,0:T(8,128)}) all-reduce(f32[16,128]{1,0:T(8,128)S(1)} %bitcast.222, f32[16,128]{1,0:T(8,128)S(1)} %bitcast.223), channel_id=1, replica_groups=mesh['ctx'=8,'exp'=16,'tp'=4] {'exp','tp'}, use_global_device_ids=true, to_apply=%region_26.27 | all-reduce | flops 4096 | bytes 32768 | tf_op jit(solution)/shard_map/psum | solution.py:118
  1007.7 6.0 broadcast_multiply_fusion
  1013.7 7.4 mul.423
  1021.1 4.2 fusion.57
  (444 shorter events, 164.4 us)
Async XLA Ops:
  7.2 554.9 %copy-start = (bf16[1,224,4096]{2,1,0:T(8,128)(2,1)S(1)}, bf16[1,224,4096]{2,1,0:T(8,128)(2,1)}, u32[]{:S(2)}) copy-start(bf16[1,224,4096]{2,1,0:T(8,128)(2,1)} %param.39) | copy-start | bytes 5505028
  7.2 204.4 %all-gather.2.cloned.1.call-start = ((), (), s32[]{:S(2)}) async-start(), calls=%async_computation.4 | async-start | bytes 1179648 | tf_op jit(solution)/shard_map/all_gather | solution.py:122
  7.9 282.1 %reduce-scatter.2.cloned.1.call-start = ((), (), s32[]{:S(2)}) async-start(), calls=%async_computation.5 | async-start | bytes 1114112 | tf_op jit(solution)/shard_map/reduce_scatter | solution.py:125
  38.9 5.0 collective-permute-start.1
  43.9 5.0 collective-permute-start.1
  48.9 5.0 collective-permute-start.1
  53.8 5.0 collective-permute-start.1
  58.8 5.0 collective-permute-start.1
  63.8 5.0 collective-permute-start.1
  68.7 5.0 collective-permute-start.1
  74.8 30.2 %copy-start.6 = (bf16[128,128]{1,0:T(8,128)(2,1)S(1)}, bf16[128,128]{1,0:T(8,128)(2,1)}, u32[]{:S(2)}) copy-start(bf16[128,128]{1,0:T(8,128)(2,1)} %param.33) | copy-start | bytes 98308
  74.8 30.2 %copy-start.9 = (f32[16,128]{1,0:T(8,128)S(1)}, f32[16,128]{1,0:T(8,128)}, u32[]{:S(2)}) copy-start(f32[16,128]{1,0:T(8,128)} %param.30) | copy-start | bytes 24580
  137.8 3.3 collective-permute-start
  141.0 5.0 collective-permute-start
  146.0 5.0 collective-permute-start
  151.0 5.0 collective-permute-start
  155.9 5.0 collective-permute-start
  160.9 5.0 collective-permute-start
  165.9 5.0 collective-permute-start
  207.9 1.6 copy-start.3
  208.0 1.5 copy-start.2
  208.0 1.5 copy-start.8
  209.5 2.0 copy-start.12
  211.5 2.8 copy-start.10
  211.5 134.9 %copy-start.7 = (bf16[8,4096]{1,0:T(8,128)(2,1)S(1)}, bf16[8,4096]{1,0:T(8,128)(2,1)}, u32[]{:S(2)}) copy-start(bf16[8,4096]{1,0:T(8,128)(2,1)} %param.35) | copy-start | bytes 196612
  211.5 136.2 %copy-start.5 = (bf16[128,128]{1,0:T(8,128)(2,1)}, bf16[128,128]{1,0:T(8,128)(2,1)S(1)}, u32[]{:S(2)}) copy-start(bf16[128,128]{1,0:T(8,128)(2,1)S(1)} %get-tuple-element.581) | copy-start | bytes 98308
  214.2 132.1 %all-reduce.4.cloned.1.call-start = ((), (), s32[]{:S(2)}) async-start(), calls=%async_computation.6 | async-start | bytes 131072 | tf_op jit(solution)/shard_map/psum | solution.py:128
  351.8 202.9 %all-to-all-start = ((bf16[128,3,4096]{2,1,0:T(4,128)(2,1)}), bf16[128,3,4096]{2,1,0:T(4,128)(2,1)}, u32[]{:S(2)}, u32[]{:S(2)}) async-start(bf16[128,3,4096]{2,1,0:T(4,128)(2,1)} %bitcast.205), calls=%async_computation.1 | async-start | bytes 8388608 | tf_op jit(solution)/shard_map/all_to_all | solution.py:162
  369.3 192.8 %copy-start.4 = (bf16[1,224,384]{2,1,0:T(8,128)(2,1)S(1)}, bf16[1,224,384]{2,1,0:T(8,128)(2,1)}, u32[]{:S(2)}) copy-start(bf16[1,224,384]{2,1,0:T(8,128)(2,1)} %param.38) | copy-start | bytes 516100
  562.1 147.8 %copy-start.11 = (f32[8,2]{0,1:T(2,128)S(1)}, f32[8,2]{0,1:T(2,128)}, u32[]{:S(2)}) copy-start(f32[8,2]{0,1:T(2,128)} %param.37) | copy-start | bytes 196
  677.2 32.9 %all-to-all-start.2 = ((f32[16,1,3]{2,1,0:T(1,128)}), f32[16,1,3]{2,1,0:T(1,128)S(1)}, u32[]{:S(2)}, u32[]{:S(2)}) async-start(f32[16,1,3]{2,1,0:T(1,128)} %bitcast.55), calls=%async_computation.3 | async-start | bytes 16384 | tf_op jit(solution)/shard_map/all_to_all | solution.py:182
  712.6 294.4 %all-to-all-start.1 = ((bf16[128,1,3]{2,1,0:T(2,128)(2,1)}), bf16[128,1,3]{2,1,0:T(2,128)(2,1)S(1)}, u32[]{:S(2)}, u32[]{:S(2)}) async-start(bf16[128,1,3]{2,1,0:T(2,128)(2,1)} %copy.71), calls=%async_computation.2 | async-start | bytes 131072 | tf_op jit(solution)/shard_map/all_to_all | solution.py:163
  (1 other events, 1.5 us)
Sparse Core Ops, SparseCore 0:
  10.2 33.9 all-gather.1
  214.3 75.6 reduce-scatter.1
  292.4 53.8 all-reduce.3
where the time goes:
time: 1040 us; the launch traced here: 1030 us
  blocking collectives  410 us (39%)
  waiting for transfers between devices  348 us (33%)
  starting transfers between devices  82 us (8%)
  local copies, waits for them, and re-layouts  77.2 us (7%)
  other arithmetic  76.7 us (7%)
  between operations  14.7 us (1%)
  loops' own time  12.8 us (1%)
  matrix products  11.1 us (1%)
    psum x1, blocking collectives, shards(): lax.psum((in_part, out_part), ('exp', 'tp'))  276 us
    all_to_all x1, waiting for transfers between devices, shards(): lax.all_to_all(wide_rows, ('ctx', 'exp'), split_axis=0, concat_axis=0, ti...  185 us
    psum x1, blocking collectives, shards(): totals = lax.psum(totals_part, ('ctx', 'tp'))  111 us
    reduce_scatter x1, waiting for transfers between devices, shards(): lax.psum_scatter(token_part.astype(jnp.bfloat16), 'exp', scatter_dimensio...  75.1 us
    psum x1, waiting for transfers between devices, shards(): token_sum = lax.psum(token_rows, 'tp').astype(jnp.float32)  56.3 us
    ppermute x14, starting transfers between devices, from_behind(): return lax.ppermute(shard, axis, pairs)  36.9 us
    ppermute x14, waiting for transfers between devices, from_behind(): return lax.ppermute(shard, axis, pairs)  30.7 us
    psum x1, blocking collectives, shards(): decay_grad, skip_grad = lax.psum((decay_part, skip_part), 'ctx')  23.1 us
  transfers between devices with their start and end apart: 20, of which 17 were waited for; matrix products, arithmetic and copies ran while one was open for 12% of the time, Pallas kernels for 0%

commit v1 on v0

v1 whole, which is shorter than its diff:
```python
import jax
import jax.numpy as jnp
from jax import lax
from jax.experimental import pallas as pl
from jax.experimental.pallas import tpu as pltpu
from jax.sharding import PartitionSpec as P

F32 = jnp.float32
BF16 = jnp.bfloat16
MESH = pl.DeviceIdType.MESH

TOK = 128
CH = 128
NS = 16
BLK = 8
NBLK = TOK // BLK
Y, CORES, Z, X = 4, 2, 16, 4
CTX = Y * CORES
FSL = 512
CAP = 3
HALF = Z * CAP
SLOTS = CTX * HALF
NEAR = (1, 15, 2)
FAR = (4, 12, 8)


def nt(a, b):
    return lax.dot_general(a, b, (((1,), (1,)), ((), ())), preferred_element_type=F32)


def mm(a, b):
    return jnp.dot(a, b, preferred_element_type=F32)


def iota(shape, dim):
    return lax.broadcasted_iota(jnp.int32, shape, dim)


class Links:
    def __init__(self, send, recv):
        self.send, self.recv = send, recv
        self.n_send = self.n_recv = 0
        self.started = []

    def slot(self, n=1):
        first = self.n_recv
        self.n_recv += n
        assert self.n_recv <= NSEM
        return first

    def put(self, src, dst, recv_index, **device):
        copy = pltpu.make_async_remote_copy(
            src_ref=src,
            dst_ref=dst,
            send_sem=self.send.at[self.n_send],
            recv_sem=self.recv.at[recv_index],
            device_id=device,
            device_id_type=MESH,
        )
        self.n_send += 1
        assert self.n_send <= NSEM
        copy.start()
        self.started.append(copy)
        return copy

    def got(self, dst, recv_index):
        pltpu.make_async_copy(dst, dst, self.recv.at[recv_index]).wait()

    def drain(self):
        for copy in self.started:
            copy.wait_send()
        self.started = []


NSEM = 128


def body(
    x_ref, step_ref, rates_ref, inp_ref, outp_ref, skip_ref, doc_ref, g_ref, wmix_ref, resid_ref,
    idx_ref, prob_ref, hidden_ref, weight_ref,
    ssm_ref, stepg_ref, inpg_ref, outpg_ref, decg_ref, skipg_ref, slot_ref, down_ref, probg_ref,
    xf, gf, a_s, inf_s, adj_s, ap_s, bsel, ssm_f, xbuf, sbuf, wbuf, pbuf, rbuf1, abuf, rbuf2,
    gbuf, ibuf, pair_out, pair_in, sel_s, scale_s, scale_in, rows, w_s,
    iop, iop_in, iop_far, iop_near, iop_all, dsp, dsp_in, tot, tot_x, tot_c, tot_z,
    send_sems, recv_sems, local_sems, weight_sem,
):
    links = Links(send_sems, recv_sems)
    c, e, t = lax.axis_index("ctx"), lax.axis_index("exp"), lax.axis_index("tp")
    y, core = lax.div(c, 2), lax.rem(c, 2)
    r0, q0 = lax.rem(e, 4), lax.div(e, 4)
    fs = 2 * lax.rem(t + y, 4) + core

    def at_y(dy):
        return 2 * lax.rem(y + dy, 4) + core

    def at_x(dx):
        return lax.rem(t + dx, 4)

    def at_z(dz):
        return lax.rem(e + dz, Z)

    barrier = pltpu.get_barrier_semaphore()
    partners = 0
    for dc in range(CTX):
        for dx in range(X):
            if dc or dx:
                pl.semaphore_signal(
                    barrier, inc=1, device_id={"ctx": lax.rem(c + dc, CTX), "tp": at_x(dx)}, device_id_type=MESH
                )
                partners += 1
    for dz in range(1, Z):
        pl.semaphore_signal(barrier, inc=1, device_id={"exp": at_z(dz)}, device_id_type=MESH)
        partners += 1

    load_weight = pltpu.make_async_copy(weight_ref, w_s, local_sems.at[0])
    load_weight.start()
    pl.semaphore_wait(barrier, partners)

    for dy in range(4):
        if dy == 0:
            @pl.when(t == 0)
            def _():
                pltpu.make_async_copy(wmix_ref, wbuf.at[0], weight_sem.at[0]).start()

            @pl.when(t != 0)
            def _():
                pltpu.make_async_remote_copy(
                    src_ref=wmix_ref, dst_ref=wbuf.at[t], send_sem=local_sems.at[1], recv_sem=weight_sem.at[t],
                    device_id={"tp": 0}, device_id_type=MESH,
                ).start()
        else:
            copy = pltpu.make_async_remote_copy(
                src_ref=wmix_ref, dst_ref=wbuf.at[t], send_sem=send_sems.at[links.n_send],
                recv_sem=weight_sem.at[t], device_id={"ctx": at_y(dy), "tp": (4 - dy) % 4}, device_id_type=MESH,
            )
            links.n_send += 1
            copy.start()
            links.started.append(copy)

    lane8 = iota((BLK, 128), 1)
    idx = idx_ref[...].astype(F32)
    prob = prob_ref[...].astype(BF16).astype(F32)
    info = jnp.where(
        lane8 == 0, idx[:, 0:1], jnp.where(lane8 == 1, idx[:, 1:2], jnp.where(lane8 == 2, prob[:, 0:1], prob[:, 1:2]))
    )
    other_fs = 2 * lax.rem(t + y, 4) + (1 - core)
    pair_out[:, 0:FSL] = resid_ref[:, pl.ds(pl.multiple_of(other_fs * FSL, FSL), FSL)].astype(F32)
    pair_out[:, FSL:] = info
    k_pair = links.slot()
    links.put(pair_out, pair_in, k_pair, ctx=2 * y + (1 - core))

    xf[...] = x_ref[...].astype(F32)
    gf[...] = g_ref[...].astype(F32)
    g_bf = g_ref[...]
    u_bf = (step_ref[...] * xf[...]).astype(BF16)
    row, lane = iota((128, 128), 0), iota((128, 128), 1)
    b_tile = jnp.concatenate([inp_ref[...]] * BLK, axis=0)
    c_tile = jnp.concatenate([outp_ref[...]] * BLK, axis=0)
    bsel[...] = jnp.where(lax.rem(row, BLK) == lax.div(lane, NS), b_tile.T, 0.0)
    row_tok = lax.div(row, NS)

    def prepare(i, carry):
        at = pl.ds(pl.multiple_of(i * BLK, BLK), BLK)
        here = lane == row_tok + i * BLK
        decays = jnp.exp(step_ref[at, :][:, None, :] * rates_ref[...][None])
        for j in range(BLK):
            keep = (1 - doc_ref[i * BLK + j]).astype(F32)
            a_s[i * BLK + j] = decays[j] * keep
        inf_s[at] = mm(jnp.where(here, b_tile, 0.0).astype(BF16), u_bf).reshape(BLK, NS, CH)
        adj_s[at] = mm(jnp.where(here, c_tile, 0.0).astype(BF16), g_bf).reshape(BLK, NS, CH)
        return carry

    lax.fori_loop(0, NBLK, prepare, 0)

    zero = jnp.zeros((NS, CH), F32)

    def summarise(i, carry):
        state, back, damp = carry
        for j in range(BLK):
            up = i * BLK + j
            down = TOK - 1 - up
            decay = a_s[up]
            state = decay * state + inf_s[up]
            damp = damp * decay
            back = a_s[down] * (adj_s[down] + back)
        return state, back, damp

    state, back, damp = lax.fori_loop(0, NBLK, summarise, (zero, zero, zero + 1.0))
    xbuf[0, 0:NS] = damp
    xbuf[0, NS : 2 * NS] = state
    xbuf[0, 2 * NS :] = back
    k_ctx = links.slot(CTX)
    for dc in range(1, CTX):
        links.put(xbuf.at[0], xbuf.at[dc], k_ctx + dc, ctx=lax.rem(c + dc, CTX))

    links.got(pair_in, k_pair)
    mine = info
    theirs = pair_in[:, FSL:]
    first = core == 0
    ibuf[r0, q0, 0:BLK] = jnp.where(first, mine, theirs)
    ibuf[r0, q0, BLK:] = jnp.where(first, theirs, mine)
    k_ifar = links.slot(3)
    for n, dz in enumerate(FAR):
        links.put(ibuf.at[r0, q0], ibuf.at[r0, q0], k_ifar + n, exp=at_z(dz))

    for dc in range(1, CTX):
        links.got(xbuf.at[dc], k_ctx + dc)
    entering, arriving = zero, zero
    for other in range(CTX):
        from_slot = lax.rem(c - other + CTX, CTX)
        entering = jnp.where(
            other < c, xbuf[from_slot, 0:NS] * entering + xbuf[from_slot, NS : 2 * NS], entering
        )
    for other in reversed(range(CTX)):
        from_slot = lax.rem(c - other + CTX, CTX)
        arriving = jnp.where(other > c, xbuf[from_slot, 0:NS] * arriving + xbuf[from_slot, 2 * NS :], arriving)

    def scan(i, carry):
        state, back = carry
        for j in range(BLK):
            up = i * BLK + j
            down = TOK - 1 - up
            kept = a_s[up] * state
            ap_s[up] = kept
            state = kept + inf_s[up]
            adjoint = adj_s[down] + back
            adj_s[down] = adjoint
            back = a_s[down] * adjoint
        return state, back

    lax.fori_loop(0, NBLK, scan, (entering, arriving))

    for n, dz in enumerate(FAR):
        links.got(ibuf.at[r0, lax.rem(q0 + 4 - dz // 4, 4)], k_ifar + n)
    k_inear = links.slot(3)
    for n, dz in enumerate(NEAR):
        links.put(ibuf.at[r0], ibuf.at[r0], k_inear + n, exp=at_z(dz))

    rates = rates_ref[...]
    ones8 = jnp.where(iota((BLK, 128), 0) == lax.div(lane8, NS), 1.0, 0.0).astype(BF16)
    tok3, lane3 = iota((BLK, NS, 128), 0), iota((BLK, NS, 128), 2)
    skip = skip_ref[...]

    def gradients(i, carry):
        acc_in, acc_out, acc_decay = carry
        at = pl.ds(pl.multiple_of(i * BLK, BLK), BLK)
        adjoint, kept = adj_s[at], ap_s[at]
        states = (kept + inf_s[at]).reshape(128, CH).astype(BF16)
        adjoint_bf = adjoint.reshape(128, CH).astype(BF16)
        here = lane3 == tok3 + i * BLK
        acc_out += jnp.sum(jnp.where(here, nt(states, g_bf).reshape(BLK, NS, 128), 0.0), axis=0)
        acc_in += jnp.sum(jnp.where(here, nt(adjoint_bf, u_bf).reshape(BLK, NS, 128), 0.0), axis=0)
        through = mm(bsel[at, :].astype(BF16), adjoint_bf)
        product = adjoint * kept
        rated = mm(ones8, (product * rates[None]).reshape(128, CH).astype(BF16))
        step = step_ref[at, :]
        acc_decay += jnp.sum(product * step[:, None, :], axis=0)
        stepg_ref[at, :] = rated + xf[at, :] * through
        ssm_f[at, :] = skip * gf[at, :] + step * through
        return acc_in, acc_out, acc_decay

    acc_in, acc_out, acc_decay = lax.fori_loop(0, NBLK, gradients, (zero, zero, zero))

    ssm_bf = ssm_f[...].astype(BF16)
    ssm_ref[...] = ssm_bf
    sbuf[0, 0] = ssm_bf
    k_s = links.slot(2 * X)
    for dk in range(2):
        for dx in range(X):
            if dk or dx:
                links.put(
                    sbuf.at[0, 0], sbuf.at[dk, dx], k_s + dk * X + dx,
                    ctx=2 * y + lax.rem(core + dk, 2), tp=at_x(dx),
                )

    iop[0:2] = acc_in.reshape(2, 8, 128)
    iop[2:4] = acc_out.reshape(2, 8, 128)
    k_iox = links.slot(4)
    for dx in range(1, X):
        links.put(iop.at[at_x(dx)], iop_in.at[dx], k_iox + dx, tp=at_x(dx))
    dsp[0:NS] = acc_decay
    skip_part = jnp.sum(gf[...] * xf[...], axis=0, keepdims=True)
    dsp[NS:] = jnp.broadcast_to(skip_part, (BLK, CH))
    k_dsp = links.slot(CTX)
    for dc in range(1, CTX):
        links.put(dsp, dsp_in.at[dc], k_dsp + dc, ctx=lax.rem(c + dc, CTX))

    for n, dz in enumerate(NEAR):
        links.got(ibuf.at[lax.rem(r0 + 16 - dz, 4)], k_inear + n)
    infos = ibuf[...].reshape(256, 128)
    e_f = e.astype(F32)
    hit0 = jnp.where(infos[:, 0:1] == e_f, 1.0, 0.0)
    hit1 = jnp.where(infos[:, 1:2] == e_f, 1.0, 0.0)
    hit = jnp.broadcast_to(hit0 + hit1, (256, 128))
    factor = hit0 * infos[:, 2:3] + hit1 * infos[:, 3:4]
    r256, l256 = iota((256, 256), 0), iota((256, 256), 1)
    before = jnp.where((lax.div(r256, BLK) == lax.div(l256, BLK)) & (r256 > l256), 1.0, 0.0).astype(BF16)
    position = mm(before, hit.astype(BF16))
    tok_row = iota((256, 128), 0)
    tok_r, tok_q = lax.div(tok_row, 64), lax.rem(lax.div(tok_row, 16), 4)
    tok_k = lax.rem(lax.div(tok_row, BLK), 2)
    tok_slot = (tok_k * Z + tok_q * 4 + tok_r) * CAP
    slot_of = tok_slot.astype(F32) + position
    picked = jnp.where(iota((256, 128), 1).astype(F32) == slot_of, hit, 0.0)
    sel_s[...] = picked.T.astype(BF16)
    own_scale = jnp.sum(picked * factor, axis=0, keepdims=True)[:, 0 : 2 * HALF]
    zeros96 = jnp.zeros((1, 2 * HALF), F32)
    scale_s[0] = jnp.concatenate([jnp.where(y == n, own_scale, zeros96) for n in range(Y)], axis=1)
    k_scale = links.slot(4)
    for dy in range(1, 4):
        links.put(scale_s.at[0], scale_in.at[dy], k_scale + dy, ctx=at_y(dy))

    for n in range(4):
        pltpu.make_async_copy(wbuf.at[n], wbuf.at[n], weight_sem.at[n]).wait()
    for dk in range(2):
        for dx in range(X):
            if dk or dx:
                links.got(sbuf.at[dk, dx], k_s + dk * X + dx)
    mixer = wbuf[...].reshape(4 * 128, FSL)
    parts = []
    for k in range(2):
        dk = lax.rem(core + k, 2)
        lhs = jnp.concatenate([sbuf[dk, lax.rem(t - n + 4, 4)] for n in range(4)], axis=1)
        parts.append(mm(lhs, mixer).reshape(Z, BLK, FSL))
    chunks = jnp.concatenate(parts, axis=1).astype(BF16)
    for n in range(Z):
        pbuf[n % 4, n // 4] = chunks[n]

    k_r1 = links.slot(3)
    for n, dz in enumerate(NEAR):
        links.put(pbuf.at[lax.rem(r0 + dz, 4)], rbuf1.at[n], k_r1 + n, exp=at_z(dz))
    for dx in range(1, X):
        links.got(iop_in.at[dx], k_iox + dx)
    iop_far[0] = iop[t] + iop_in[1] + iop_in[2] + iop_in[3]
    k_iof = links.slot(4)
    for n, dz in enumerate(FAR):
        links.put(iop_far.at[0], iop_far.at[n + 1], k_iof + n, exp=at_z(dz))
    for n in range(3):
        links.got(rbuf1.at[n], k_r1 + n)
    summed = pbuf[r0].astype(F32)
    for n in range(3):
        summed += rbuf1[n].astype(F32)
    abuf[...] = summed.astype(BF16)
    k_r2 = links.slot(3)
    for n, dz in enumerate(FAR):
        links.put(abuf.at[lax.rem(q0 + dz // 4, 4)], rbuf2.at[n], k_r2 + n, exp=at_z(dz))
    own_resid = resid_ref[:, pl.ds(pl.multiple_of(fs * FSL, FSL), FSL)].astype(F32)
    their_resid = pair_in[:, 0:FSL]
    resid = jnp.concatenate(
        [jnp.where(first, own_resid, their_resid), jnp.where(first, their_resid, own_resid)], axis=0
    )
    for n in range(3):
        links.got(rbuf2.at[n], k_r2 + n)
    total = abuf[q0].astype(F32) + resid
    for n in range(3):
        total += rbuf2[n].astype(F32)

    gbuf[r0, q0] = total.astype(BF16)
    k_g1 = links.slot(3)
    for n, dz in enumerate(FAR):
        links.put(gbuf.at[r0, q0], gbuf.at[r0, q0], k_g1 + n, exp=at_z(dz))
    for n in range(3):
        links.got(iop_far.at[n + 1], k_iof + n)
    iop_near[0] = iop_far[0] + iop_far[1] + iop_far[2] + iop_far[3]
    for n, dz in enumerate(FAR):
        links.got(gbuf.at[r0, lax.rem(q0 + 4 - dz // 4, 4)], k_g1 + n)
    k_g2 = links.slot(3)
    for n, dz in enumerate(NEAR):
        links.put(gbuf.at[r0], gbuf.at[r0], k_g2 + n, exp=at_z(dz))
    k_ion = links.slot(4)
    for n, dz in enumerate(NEAR):
        links.put(iop_near.at[0], iop_near.at[n + 1], k_ion + n, exp=at_z(dz))
    for n, dz in enumerate(NEAR):
        links.got(gbuf.at[lax.rem(r0 + 16 - dz, 4)], k_g2 + n)

    picked_rows = mm(sel_s[...], gbuf[...].reshape(256, FSL)).astype(BF16)
    rows[core, t, y, 0] = picked_rows[0:HALF]
    rows[core, t, y, 1] = picked_rows[HALF : 2 * HALF]
    other_core = 2 * y + (1 - core)
    k_p1 = links.slot(8)
    for d in (1, 3, 2):
        links.put(rows.at[core, t, y, 0], rows.at[core, t, y, 0], k_p1 + d, tp=at_x(d))
        links.put(rows.at[core, t, y, 1], rows.at[core, t, y, 1], k_p1 + 4 + d, ctx=at_y(d))
    for d in (1, 3, 2):
        links.got(rows.at[core, at_x(4 - d), y, 0], k_p1 + d)
        links.got(rows.at[core, t, lax.rem(y + 4 - d, 4), 1], k_p1 + 4 + d)
    k_p2 = links.slot(8)
    for d in (1, 3, 2):
        links.put(rows.at[core, :, y, 0], rows.at[core, :, y, 0], k_p2 + d, ctx=at_y(d))
        links.put(rows.at[core, t, :, 1], rows.at[core, t, :, 1], k_p2 + 4 + d, tp=at_x(d))
    k_core = links.slot(8)
    links.put(rows.at[core, :, y, 0], rows.at[core, :, y, 0], k_core, ctx=other_core)
    links.put(rows.at[core, t, :, 1], rows.at[core, t, :, 1], k_core + 4, ctx=other_core)

    for n in range(3):
        links.got(iop_near.at[n + 1], k_ion + n)
    iop_out = iop_near[0] + iop_near[1] + iop_near[2] + iop_near[3]
    iop_in[0] = iop_out
    k_ioa = links.slot(4)
    for dx in range(1, X):
        links.put(iop_in.at[0], iop_all.at[t], k_ioa + dx, tp=at_x(dx))
    for dc in range(1, CTX):
        links.got(dsp_in.at[dc], k_dsp + dc)
    sums = dsp[...]
    for dc in range(1, CTX):
        sums += dsp_in[dc]
    decg_ref[...] = sums[0:NS]
    skipg_ref[...] = sums[NS : NS + 1]
    for dy in range(1, 4):
        links.got(scale_in.at[dy], k_scale + dy)
    scale = scale_s[0] + scale_in[1] + scale_in[2] + scale_in[3]

    hidden = hidden_ref[...]
    hidden_scaled = (hidden.astype(F32) * scale).astype(BF16)
    load_weight.wait()

    for d in (1, 3, 2):
        from_y, from_x = lax.rem(y + 4 - d, 4), at_x(4 - d)
        links.got(rows.at[core, :, from_y, 0], k_p2 + d)
        links.put(rows.at[core, :, from_y, 0], rows.at[core, :, from_y, 0], k_core + d, ctx=other_core)
        links.got(rows.at[core, from_x, :, 1], k_p2 + 4 + d)
        links.put(rows.at[core, from_x, :, 1], rows.at[core, from_x, :, 1], k_core + 4 + d, ctx=other_core)
    theirs_core = 1 - core
    for d in (0, 1, 3, 2):
        from_y, from_x = lax.rem(y + 4 - d, 4), at_x(4 - d)
        links.got(rows.at[theirs_core, :, from_y, 0], k_core + d)
        links.got(rows.at[theirs_core, from_x, :, 1], k_core + 4 + d)

    direct = jnp.zeros((hidden.shape[0], SLOTS), F32)
    for k in range(2):
        for f in range(4):
            at = pl.ds((2 * f + k) * FSL, FSL)
            part = jnp.concatenate([rows[k, (f - n) % 4, n].reshape(2 * HALF, FSL) for n in range(Y)], axis=0)
            direct += nt(w_s[:, at], part)
            down_ref[:, at] = mm(hidden_scaled, part).astype(BF16)
    slot_ref[...] = (direct * scale).astype(BF16)
    tot[0] = jnp.sum(hidden.astype(F32) * direct, axis=0, keepdims=True)

    k_tx = links.slot(4)
    for dx in range(1, X):
        links.put(tot.at[0], tot_x.at[dx], k_tx + dx, tp=at_x(dx))
    for dx in range(1, X):
        links.got(iop_all.at[at_x(4 - dx)], k_ioa + dx)
    iop_all[t] = iop_out
    inpg_ref[...] = iop_all[0:2].reshape(NS, 128)
    outpg_ref[...] = iop_all[2:4].reshape(NS, 128)

    idx0, idx1 = jnp.broadcast_to(info[:, 0:1], (BLK, 128)), jnp.broadcast_to(info[:, 1:2], (BLK, 128))
    rows8 = iota((BLK, 128), 0)
    pos0, pos1 = jnp.zeros((BLK, 128), F32), jnp.zeros((BLK, 128), F32)
    for i in range(BLK):
        i0, i1 = idx0[i : i + 1], idx1[i : i + 1]
        pos0 += jnp.where((rows8 > i) & ((i0 == idx0) | (i1 == idx0)), 1.0, 0.0)
        pos1 += jnp.where((rows8 > i) & ((i0 == idx1) | (i1 == idx1)), 1.0, 0.0)
    lane384 = iota((BLK, SLOTS), 1).astype(F32)
    base = ((c * Z + e) * CAP).astype(F32)

    for dx in range(1, X):
        links.got(tot_x.at[dx], k_tx + dx)
    tot_c[0] = tot[0] + tot_x[1] + tot_x[2] + tot_x[3]
    k_tc = links.slot(CTX)
    for dc in range(1, CTX):
        links.put(tot_c.at[0], tot_c.at[dc], k_tc + dc, ctx=lax.rem(c + dc, CTX))
    for dc in range(1, CTX):
        links.got(tot_c.at[dc], k_tc + dc)
    plane = tot_c[0]
    for dc in range(1, CTX):
        plane += tot_c[dc]
    tot_z[0] = plane
    k_tz = links.slot(Z)
    for dz in range(1, Z):
        links.put(tot_z.at[0], tot_z.at[dz], k_tz + dz, exp=at_z(dz))
    for dz in range(1, Z):
        links.got(tot_z.at[dz], k_tz + dz)
    val0, val1 = jnp.zeros((BLK, SLOTS), F32), jnp.zeros((BLK, SLOTS), F32)
    for dz in range(Z):
        expert = at_z(Z - dz).astype(F32)
        line = jnp.broadcast_to(tot_z[dz], (BLK, SLOTS))
        val0 = jnp.where(info[:, 0:1] == expert, line, val0)
        val1 = jnp.where(info[:, 1:2] == expert, line, val1)
    out0 = jnp.sum(jnp.where(lane384 == base + pos0[:, 0:1], val0, 0.0), axis=1, keepdims=True)
    out1 = jnp.sum(jnp.where(lane384 == base + pos1[:, 0:1], val1, 0.0), axis=1, keepdims=True)
    probg_ref[...] = jnp.where(iota((BLK, 2), 1) == 0, out0, out1)

    @pl.when(t != 0)
    def _():
        pltpu.make_async_copy(wmix_ref, wbuf.at[0], local_sems.at[1]).wait()

    links.drain()


def shards(
    mixer_input, step_sizes, decay_rates, input_proj, output_proj, skip_gain, doc_starts, ssm_grad, mixer_in_weight,
    residual_grad, expert_index_pairs, route_probs, hidden_saved, down_weight,
):
    hidden = hidden_saved[0].shape[0]
    features = down_weight.shape[2]
    vmem = pl.BlockSpec(memory_space=pltpu.VMEM)
    anywhere = pl.BlockSpec(memory_space=pl.ANY)
    smem = pl.BlockSpec(memory_space=pltpu.SMEM)
    shape = jax.ShapeDtypeStruct
    out = pl.pallas_call(
        body,
        out_shape=(
            shape((TOK, CH), BF16),
            shape((TOK, CH), F32),
            shape((NS, TOK), F32),
            shape((NS, TOK), F32),
            shape((NS, CH), F32),
            shape((1, CH), F32),
            shape((hidden, SLOTS), BF16),
            shape((hidden, features), BF16),
            shape((BLK, 2), F32),
        ),
        in_specs=[vmem, vmem, vmem, vmem, vmem, vmem, smem, vmem, anywhere, vmem, vmem, vmem, vmem, anywhere],
        out_specs=tuple([vmem] * 9),
        scratch_shapes=[
            pltpu.VMEM((TOK, CH), F32),
            pltpu.VMEM((TOK, CH), F32),
            pltpu.VMEM((TOK, NS, CH), F32),
            pltpu.VMEM((TOK, NS, CH), F32),
            pltpu.VMEM((TOK, NS, CH), F32),
            pltpu.VMEM((TOK, NS, CH), F32),
            pltpu.VMEM((128, 128), F32),
            pltpu.VMEM((TOK, CH), F32),
            pltpu.VMEM((CTX, 3 * NS, CH), F32),
            pltpu.VMEM((2, X, TOK, CH), BF16),
            pltpu.VMEM((4, 128, FSL), BF16),
            pltpu.VMEM((4, 4, 16, FSL), BF16),
            pltpu.VMEM((3, 4, 16, FSL), BF16),
            pltpu.VMEM((4, 16, FSL), BF16),
            pltpu.VMEM((3, 16, FSL), BF16),
            pltpu.VMEM((4, 4, 16, FSL), BF16),
            pltpu.VMEM((4, 4, 16, 128), F32),
            pltpu.VMEM((BLK, FSL + 128), F32),
            pltpu.VMEM((BLK, FSL + 128), F32),
            pltpu.VMEM((128, 256), BF16),
            pltpu.VMEM((1, 1, SLOTS), F32),
            pltpu.VMEM((4, 1, SLOTS), F32),
            pltpu.VMEM((2, X, Y, 2, HALF, FSL), BF16),
            pltpu.VMEM((hidden, features), BF16),
            pltpu.VMEM((4, 8, 128), F32),
            pltpu.VMEM((4, 8, 128), F32),
            pltpu.VMEM((4, 8, 128), F32),
            pltpu.VMEM((4, 8, 128), F32),
            pltpu.VMEM((4, 8, 128), F32),
            pltpu.VMEM((NS + BLK, CH), F32),
            pltpu.VMEM((CTX, NS + BLK, CH), F32),
            pltpu.VMEM((1, 1, SLOTS), F32),
            pltpu.VMEM((4, 1, SLOTS), F32),
            pltpu.VMEM((CTX, 1, SLOTS), F32),
            pltpu.VMEM((Z, 1, SLOTS), F32),
            pltpu.SemaphoreType.DMA((NSEM,)),
            pltpu.SemaphoreType.DMA((NSEM,)),
            pltpu.SemaphoreType.DMA((2,)),
            pltpu.SemaphoreType.DMA((4,)),
        ],
        compiler_params=pltpu.CompilerParams(
            collective_id=0, has_side_effects=True, vmem_limit_bytes=48 * 1024 * 1024
        ),
        name="scan_and_experts",
    )(
        mixer_input, step_sizes, decay_rates, input_proj, output_proj, skip_gain.reshape(1, CH), doc_starts, ssm_grad,
        mixer_in_weight, residual_grad, expert_index_pairs, route_probs, hidden_saved[0], down_weight[0],
    )
    ssm, stepg, inpg, outpg, decg, skipg, slot, down, probg = out
    return ssm, stepg, inpg, outpg, decg, skipg.reshape(CH), slot[None], down[None], probg


def solution(mesh):
    return jax.shard_map(
        shards,
        mesh=mesh,
        in_specs=(
            P("ctx", ("exp", "tp")),
            P("ctx", ("exp", "tp")),
            P(None, ("exp", "tp")),
            P(None, "ctx"),
            P(None, "ctx"),
            P(("exp", "tp")),
            P("ctx"),
            P("ctx", ("exp", "tp")),
            P(("exp", "tp"), "ctx"),
            P(("ctx", "exp"), None),
            P(("ctx", "exp"), None),
            P(("ctx", "exp"), None),
            P("exp", ("ctx", "tp"), None),
            P("exp", ("ctx", "tp"), None),
        ),
        out_specs=(
            P("ctx", ("exp", "tp")),
            P("ctx", ("exp", "tp")),
            P(None, "ctx"),
            P(None, "ctx"),
            P(None, ("exp", "tp")),
            P(("exp", "tp")),
            P("exp", ("ctx", "tp"), None),
            P("exp", ("ctx", "tp"), None),
            P(("ctx", "exp"), None),
        ),
        check_vma=False,
    )
```

time: 1040 us -> 122 us (0.12)
  the two profiles are of different devices: /device:TPU:24 before, /device:TPU:1 now
where the time goes in v1:
time: 122 us; the launch traced here: 121 us
  Pallas kernels  103 us (84%)
  local copies, waits for them, and re-layouts  17.5 us (14%)
    pallas_call x1, Pallas kernels, shards(): pl.pallas_call(body, out_shape=(shape((TOK, CH), BF16), shape((TOK, CH),...  103 us
    unnamed x35, local copies, waits for them, and re-layouts  17.5 us

profile of v1, /device:TPU:1, one launch (start us, length us, event | category | flops | bytes accessed | tf_op | source)
XLA Modules:
  0.0 121.0 jit_solution(8829579787467399314)
XLA Ops:
  0.6 0.8 copy.23.idx_ref
  1.4 0.8 copy.24.prob_ref
  2.1 0.0 copy-start
  2.2 1.5 %copy-done = bf16[1,224,4096]{2,1,0:T(8,128)(2,1)S(1)} copy-done((bf16[1,224,4096]{2,1,0:T(8,128)(2,1)S(1)}, bf16[1,224,4096]{2,1,0:T(8,128)(2,1)}, u32[]{:S(2)}) %copy-start) | copy-done | bytes 1835032
  3.6 0.0 copy-start.1
  3.7 0.9 copy-done.1
  4.6 0.0 copy-start.2
  4.6 0.9 copy-done.2
  5.5 0.0 copy-start.3
  5.5 0.8 copy-done.3
  6.3 0.0 copy-start.4
  6.3 0.8 copy-done.4
  7.2 0.0 copy-start.5
  7.2 0.8 copy-done.5
  7.9 0.0 copy-start.6
  7.9 0.8 copy-done.6
  8.7 0.0 copy-start.7
  8.7 0.7 copy-done.7
  9.4 0.7 copy-done.8
  10.1 0.7 copy-done.9
  10.8 0.7 copy-done.10
  11.4 0.7 copy-done.11
  12.1 102.8 %scan_and_experts.1 = (bf16[128,128]{1,0:T(8,128)(2,1)S(1)}, f32[128,128]{1,0:T(8,128)S(1)}, f32[16,128]{1,0:T(8,128)S(1)}, f32[16,128]{1,0:T(8,128)S(1)}, f32[1...) custom-call(bf16[128,128]{1,0:T(8,128)(2,1)S(1)} %copy-done.5, ...), custom_call_target="tpu_custom_call" | custom-call | tf_op jit(solution)/shard_map/scan_and_experts/pallas_call | solution.py:502
  114.9 0.6 copy.25
  115.6 0.6 copy.34
  116.2 0.6 copy.35
  116.8 0.6 copy.36
  117.4 0.6 copy.37
  118.0 0.6 copy.38
  118.6 0.5 copy.39
  119.1 0.7 copy.40
  119.8 1.2 %copy.41 = bf16[1,224,4096]{2,1,0:T(8,128)(2,1)} copy(bf16[1,224,4096]{2,1,0:T(8,128)(2,1)S(1)} %bitcast.6) | data formatting | bytes 3670016
  (4 shorter events, 0.0 us)
Async XLA Ops:
  2.1 1.5 %copy-start = (bf16[1,224,4096]{2,1,0:T(8,128)(2,1)S(1)}, bf16[1,224,4096]{2,1,0:T(8,128)(2,1)}, u32[]{:S(2)}) copy-start(bf16[1,224,4096]{2,1,0:T(8,128)(2,1)} %param.27) | copy-start | bytes 5505028
  3.6 0.9 copy-start.1
  4.6 0.9 copy-start.2
  5.5 0.8 copy-start.3
  6.3 0.8 copy-start.4
  7.2 0.8 copy-start.5
  7.9 0.8 copy-start.6
  8.7 0.7 copy-start.7
  9.4 0.7 copy-start.8
  10.1 0.7 copy-start.9
  10.8 0.7 copy-start.10
  11.4 0.7 copy-start.11

commit v2 on v1

--- a/solution.py
+++ b/solution.py
@@ -20,7 +20,6 @@
 CAP = 3
 HALF = Z * CAP
 SLOTS = CTX * HALF
-NEAR = (1, 15, 2)
 FAR = (4, 12, 8)
 
 
@@ -72,13 +71,15 @@
         self.started = []
 
 
-NSEM = 128
+NSEM = 160
+VMEM_LIMIT = 60 * 1024 * 1024
 
 
 def body(
-    x_ref, step_ref, rates_ref, inp_ref, outp_ref, skip_ref, doc_ref, g_ref, wmix_ref, resid_ref,
-    idx_ref, prob_ref, hidden_ref, weight_ref,
-    ssm_ref, stepg_ref, inpg_ref, outpg_ref, decg_ref, skipg_ref, slot_ref, down_ref, probg_ref,
+    x_hbm, step_hbm, rates_hbm, inp_hbm, outp_hbm, skip_hbm, doc_hbm, g_hbm, wmix_ref, resid_hbm,
+    idx_hbm, prob_hbm, hidden_hbm, weight_ref,
+    ssm_ref, stepg_ref, inpg_ref, outpg_ref, decg_ref, skipg_ref, slot_ref, down_hbm, probg_ref,
+    x_ref, step_ref, rates_ref, inp_ref, outp_ref, skip_ref, doc_ref, g_ref, resid_ref, idx_ref, prob_ref, hidden_ref, down_ref,
     xf, gf, a_s, inf_s, adj_s, ap_s, bsel, ssm_f, xbuf, sbuf, wbuf, pbuf, rbuf1, abuf, rbuf2,
     gbuf, ibuf, pair_out, pair_in, sel_s, scale_s, scale_in, rows, w_s,
     iop, iop_in, iop_far, iop_near, iop_all, dsp, dsp_in, tot, tot_x, tot_c, tot_z,
@@ -112,9 +113,85 @@
         pl.semaphore_signal(barrier, inc=1, device_id={"exp": at_z(dz)}, device_id_type=MESH)
         partners += 1
 
-    load_weight = pltpu.make_async_copy(weight_ref, w_s, local_sems.at[0])
-    load_weight.start()
+    def load(src, dst, at):
+        copy = pltpu.make_async_copy(src, dst, local_sems.at[at])
+        copy.start()
+        return copy
+
+    scan_loads = [
+        load(src, dst, 2 + n)
+        for n, (src, dst) in enumerate((
+            (step_hbm, step_ref), (rates_hbm, rates_ref), (x_hbm, x_ref), (g_hbm, g_ref), (inp_hbm, inp_ref),
+            (outp_hbm, outp_ref), (doc_hbm, doc_ref), (skip_hbm, skip_ref), (idx_hbm, idx_ref),
+            (prob_hbm, prob_ref), (resid_hbm, resid_ref),
+        ))
+    ]
+    late_loads = [load(hidden_hbm, hidden_ref, 13)]
+    for n in range(7):
+        part = pl.ds(n * 32, 32)
+        late_loads.append(load(weight_ref.at[part], w_s.at[part], 14 + n))
+    near = (1, 15, 2 + 12 * core)
+    for copy in scan_loads:
+        copy.wait()
+
+    lane8 = iota((BLK, 128), 1)
+    row8 = iota((BLK, 128), 0)
+    info = jnp.zeros((BLK, 128), F32)
+    for i in range(BLK):
+        for k in range(2):
+            info = jnp.where((row8 == i) & (lane8 == k), idx_ref[k, i].astype(F32), info)
+            info = jnp.where((row8 == i) & (lane8 == 2 + k), prob_ref[k, i], info)
+    info = info.astype(BF16).astype(F32)
+    other_fs = 2 * lax.rem(t + y, 4) + (1 - core)
+    pair_out[:, 0:FSL] = resid_ref[:, pl.ds(pl.multiple_of(other_fs * FSL, FSL), FSL)].astype(F32)
+    pair_out[:, FSL:] = info
+    xf[...] = x_ref[...].astype(F32)
+    gf[...] = g_ref[...].astype(F32)
+    g_bf = g_ref[...]
+    u_bf = (step_ref[...] * xf[...]).astype(BF16)
+    row, lane = iota((128, 128), 0), iota((128, 128), 1)
+    b_tile = jnp.concatenate([inp_ref[...]] * BLK, axis=0)
+    c_tile = jnp.concatenate([outp_ref[...]] * BLK, axis=0)
+    bsel[...] = jnp.where(lax.rem(row, BLK) == lax.div(lane, NS), b_tile.T, 0.0)
+    row_tok = lax.div(row, NS)
+
+    def prepare(i, carry):
+        at = pl.ds(pl.multiple_of(i * BLK, BLK), BLK)
+        here = lane == row_tok + i * BLK
+        decays = jnp.exp(step_ref[at, :][:, None, :] * rates_ref[...][None])
+        for j in range(BLK):
+            keep = (1 - doc_ref[i * BLK + j]).astype(F32)
+            a_s[i * BLK + j] = decays[j] * keep
+        inf_s[at] = mm(jnp.where(here, b_tile, 0.0).astype(BF16), u_bf).reshape(BLK, NS, CH)
+        adj_s[at] = mm(jnp.where(here, c_tile, 0.0).astype(BF16), g_bf).reshape(BLK, NS, CH)
+        return carry
+
+    lax.fori_loop(0, NBLK, prepare, 0)
+
+    zero = jnp.zeros((NS, CH), F32)
+
+    def summarise(i, carry):
+        state, back, damp = carry
+        for j in range(BLK):
+            up = i * BLK + j
+            down = TOK - 1 - up
+            decay = a_s[up]
+            state = decay * state + inf_s[up]
+            damp = damp * decay
+            back = a_s[down] * (adj_s[down] + back)
+        return state, back, damp
+
+    state, back, damp = lax.fori_loop(0, NBLK, summarise, (zero, zero, zero + 1.0))
+    xbuf[0, 0:NS] = damp
+    xbuf[0, NS : 2 * NS] = state
+    xbuf[0, 2 * NS :] = back
     pl.semaphore_wait(barrier, partners)
+    k_ctx = links.slot(CTX)
+    for dc in range(1, CTX):
+        links.put(xbuf.at[0], xbuf.at[dc], k_ctx + dc, ctx=lax.rem(c + dc, CTX))
+
+    k_pair = links.slot()
+    links.put(pair_out, pair_in, k_pair, ctx=2 * y + (1 - core))
 
     for dy in range(4):
         if dy == 0:
@@ -137,62 +214,6 @@
             copy.start()
             links.started.append(copy)
 
-    lane8 = iota((BLK, 128), 1)
-    idx = idx_ref[...].astype(F32)
-    prob = prob_ref[...].astype(BF16).astype(F32)
-    info = jnp.where(
-        lane8 == 0, idx[:, 0:1], jnp.where(lane8 == 1, idx[:, 1:2], jnp.where(lane8 == 2, prob[:, 0:1], prob[:, 1:2]))
-    )
-    other_fs = 2 * lax.rem(t + y, 4) + (1 - core)
-    pair_out[:, 0:FSL] = resid_ref[:, pl.ds(pl.multiple_of(other_fs * FSL, FSL), FSL)].astype(F32)
-    pair_out[:, FSL:] = info
-    k_pair = links.slot()
-    links.put(pair_out, pair_in, k_pair, ctx=2 * y + (1 - core))
-
-    xf[...] = x_ref[...].astype(F32)
-    gf[...] = g_ref[...].astype(F32)
-    g_bf = g_ref[...]
-    u_bf = (step_ref[...] * xf[...]).astype(BF16)
-    row, lane = iota((128, 128), 0), iota((128, 128), 1)
-    b_tile = jnp.concatenate([inp_ref[...]] * BLK, axis=0)
-    c_tile = jnp.concatenate([outp_ref[...]] * BLK, axis=0)
-    bsel[...] = jnp.where(lax.rem(row, BLK) == lax.div(lane, NS), b_tile.T, 0.0)
-    row_tok = lax.div(row, NS)
-
-    def prepare(i, carry):
-        at = pl.ds(pl.multiple_of(i * BLK, BLK), BLK)
-        here = lane == row_tok + i * BLK
-        decays = jnp.exp(step_ref[at, :][:, None, :] * rates_ref[...][None])
-        for j in range(BLK):
-            keep = (1 - doc_ref[i * BLK + j]).astype(F32)
-            a_s[i * BLK + j] = decays[j] * keep
-        inf_s[at] = mm(jnp.where(here, b_tile, 0.0).astype(BF16), u_bf).reshape(BLK, NS, CH)
-        adj_s[at] = mm(jnp.where(here, c_tile, 0.0).astype(BF16), g_bf).reshape(BLK, NS, CH)
-        return carry
-
-    lax.fori_loop(0, NBLK, prepare, 0)
-
-    zero = jnp.zeros((NS, CH), F32)
-
-    def summarise(i, carry):
-        state, back, damp = carry
-        for j in range(BLK):
-            up = i * BLK + j
-            down = TOK - 1 - up
-            decay = a_s[up]
-            state = decay * state + inf_s[up]
-            damp = damp * decay
-            back = a_s[down] * (adj_s[down] + back)
-        return state, back, damp
-
-    state, back, damp = lax.fori_loop(0, NBLK, summarise, (zero, zero, zero + 1.0))
-    xbuf[0, 0:NS] = damp
-    xbuf[0, NS : 2 * NS] = state
-    xbuf[0, 2 * NS :] = back
-    k_ctx = links.slot(CTX)
-    for dc in range(1, CTX):
-        links.put(xbuf.at[0], xbuf.at[dc], k_ctx + dc, ctx=lax.rem(c + dc, CTX))
-
     links.got(pair_in, k_pair)
     mine = info
     theirs = pair_in[:, FSL:]
@@ -233,7 +254,7 @@
     for n, dz in enumerate(FAR):
         links.got(ibuf.at[r0, lax.rem(q0 + 4 - dz // 4, 4)], k_ifar + n)
     k_inear = links.slot(3)
-    for n, dz in enumerate(NEAR):
+    for n, dz in enumerate(near):
         links.put(ibuf.at[r0], ibuf.at[r0], k_inear + n, exp=at_z(dz))
 
     rates = rates_ref[...]
@@ -264,14 +285,11 @@
     ssm_bf = ssm_f[...].astype(BF16)
     ssm_ref[...] = ssm_bf
     sbuf[0, 0] = ssm_bf
+    other_core = 2 * y + (1 - core)
     k_s = links.slot(2 * X)
-    for dk in range(2):
-        for dx in range(X):
-            if dk or dx:
-                links.put(
-                    sbuf.at[0, 0], sbuf.at[dk, dx], k_s + dk * X + dx,
-                    ctx=2 * y + lax.rem(core + dk, 2), tp=at_x(dx),
-                )
+    for dx in (2, 1, 3):
+        links.put(sbuf.at[0, 0], sbuf.at[0, dx], k_s + dx, tp=at_x(dx))
+    links.put(sbuf.at[0, 0], sbuf.at[1, 0], k_s + X, ctx=other_core)
 
     iop[0:2] = acc_in.reshape(2, 8, 128)
     iop[2:4] = acc_out.reshape(2, 8, 128)
@@ -285,7 +303,7 @@
     for dc in range(1, CTX):
         links.put(dsp, dsp_in.at[dc], k_dsp + dc, ctx=lax.rem(c + dc, CTX))
 
-    for n, dz in enumerate(NEAR):
+    for n, dz in enumerate(near):
         links.got(ibuf.at[lax.rem(r0 + 16 - dz, 4)], k_inear + n)
     infos = ibuf[...].reshape(256, 128)
     e_f = e.astype(F32)
@@ -312,10 +330,11 @@
 
     for n in range(4):
         pltpu.make_async_copy(wbuf.at[n], wbuf.at[n], weight_sem.at[n]).wait()
-    for dk in range(2):
-        for dx in range(X):
-            if dk or dx:
-                links.got(sbuf.at[dk, dx], k_s + dk * X + dx)
+    for dx in (1, 3, 2):
+        links.got(sbuf.at[0, dx], k_s + dx)
+        links.put(sbuf.at[0, dx], sbuf.at[1, dx], k_s + X + dx, ctx=other_core)
+    for dx in (0, 1, 3, 2):
+        links.got(sbuf.at[1, dx], k_s + X + dx)
     mixer = wbuf[...].reshape(4 * 128, FSL)
     parts = []
     for k in range(2):
@@ -327,7 +346,7 @@
         pbuf[n % 4, n // 4] = chunks[n]
 
     k_r1 = links.slot(3)
-    for n, dz in enumerate(NEAR):
+    for n, dz in enumerate(near):
         links.put(pbuf.at[lax.rem(r0 + dz, 4)], rbuf1.at[n], k_r1 + n, exp=at_z(dz))
     for dx in range(1, X):
         links.got(iop_in.at[dx], k_iox + dx)
@@ -365,32 +384,50 @@
     for n, dz in enumerate(FAR):
         links.got(gbuf.at[r0, lax.rem(q0 + 4 - dz // 4, 4)], k_g1 + n)
     k_g2 = links.slot(3)
-    for n, dz in enumerate(NEAR):
+    for n, dz in enumerate(near):
         links.put(gbuf.at[r0], gbuf.at[r0], k_g2 + n, exp=at_z(dz))
     k_ion = links.slot(4)
-    for n, dz in enumerate(NEAR):
+    for n, dz in enumerate(near):
         links.put(iop_near.at[0], iop_near.at[n + 1], k_ion + n, exp=at_z(dz))
-    for n, dz in enumerate(NEAR):
+    for n, dz in enumerate(near):
         links.got(gbuf.at[lax.rem(r0 + 16 - dz, 4)], k_g2 + n)
 
     picked_rows = mm(sel_s[...], gbuf[...].reshape(256, FSL)).astype(BF16)
     rows[core, t, y, 0] = picked_rows[0:HALF]
     rows[core, t, y, 1] = picked_rows[HALF : 2 * HALF]
-    other_core = 2 * y + (1 - core)
     k_p1 = links.slot(8)
-    for d in (1, 3, 2):
+    for d in (2, 1, 3):
         links.put(rows.at[core, t, y, 0], rows.at[core, t, y, 0], k_p1 + d, tp=at_x(d))
         links.put(rows.at[core, t, y, 1], rows.at[core, t, y, 1], k_p1 + 4 + d, ctx=at_y(d))
     for d in (1, 3, 2):
         links.got(rows.at[core, at_x(4 - d), y, 0], k_p1 + d)
         links.got(rows.at[core, t, lax.rem(y + 4 - d, 4), 1], k_p1 + 4 + d)
-    k_p2 = links.slot(8)
-    for d in (1, 3, 2):
-        links.put(rows.at[core, :, y, 0], rows.at[core, :, y, 0], k_p2 + d, ctx=at_y(d))
-        links.put(rows.at[core, t, :, 1], rows.at[core, t, :, 1], k_p2 + 4 + d, tp=at_x(d))
-    k_core = links.slot(8)
-    links.put(rows.at[core, :, y, 0], rows.at[core, :, y, 0], k_core, ctx=other_core)
-    links.put(rows.at[core, t, :, 1], rows.at[core, t, :, 1], k_core + 4, ctx=other_core)
+
+    def along_y(k, from_y, h):
+        return rows.at[k, pl.ds(2 * h, 2), from_y, 0]
+
+    def along_x(k, from_x, h):
+        return rows.at[k, from_x, pl.ds(2 * h, 2), 1]
+
+    def put_y(from_y, h, slot, dy):
+        links.put(along_y(core, from_y, h), along_y(core, from_y, h), slot, ctx=at_y(dy))
+
+    def put_x(from_x, h, slot, dx):
+        links.put(along_x(core, from_x, h), along_x(core, from_x, h), slot, tp=at_x(dx))
+
+    k_p2 = links.slot(12)
+    for d, h, k in ((3, 0, 0), (1, 0, 2), (1, 1, 3), (2, 1, 5), (3, 1, 1)):
+        put_y(y, h, k_p2 + k, d)
+        put_x(t, h, k_p2 + 6 + k, d)
+    k_core = links.slot(16)
+
+    def to_core(d, h):
+        from_y, from_x = lax.rem(y + 4 - d, 4), at_x(4 - d)
+        links.put(along_y(core, from_y, h), along_y(core, from_y, h), k_core + 4 * d + h, ctx=other_core)
+        links.put(along_x(core, from_x, h), along_x(core, from_x, h), k_core + 4 * d + 2 + h, ctx=other_core)
+
+    to_core(0, 0)
+    to_core(0, 1)
 
     for n in range(3):
         links.got(iop_near.at[n + 1], k_ion + n)
@@ -410,29 +447,40 @@
         links.got(scale_in.at[dy], k_scale + dy)
     scale = scale_s[0] + scale_in[1] + scale_in[2] + scale_in[3]
 
+    late_loads[0].wait()
     hidden = hidden_ref[...]
     hidden_scaled = (hidden.astype(F32) * scale).astype(BF16)
-    load_weight.wait()
-
-    for d in (1, 3, 2):
-        from_y, from_x = lax.rem(y + 4 - d, 4), at_x(4 - d)
-        links.got(rows.at[core, :, from_y, 0], k_p2 + d)
-        links.put(rows.at[core, :, from_y, 0], rows.at[core, :, from_y, 0], k_core + d, ctx=other_core)
-        links.got(rows.at[core, from_x, :, 1], k_p2 + 4 + d)
-        links.put(rows.at[core, from_x, :, 1], rows.at[core, from_x, :, 1], k_core + 4 + d, ctx=other_core)
-    theirs_core = 1 - core
-    for d in (0, 1, 3, 2):
-        from_y, from_x = lax.rem(y + 4 - d, 4), at_x(4 - d)
-        links.got(rows.at[theirs_core, :, from_y, 0], k_core + d)
-        links.got(rows.at[theirs_core, from_x, :, 1], k_core + 4 + d)
+    for copy in late_loads[1:]:
+        copy.wait()
+
+    def got_2(d, h, k):
+        links.got(along_y(core, lax.rem(y + 4 - d, 4), h), k_p2 + k)
+        links.got(along_x(core, at_x(4 - d), h), k_p2 + 6 + k)
+
+    got_2(3, 0, 0)
+    put_y(lax.rem(y + 1, 4), 0, k_p2 + 4, 3)
+    put_x(at_x(1), 0, k_p2 + 10, 3)
+    to_core(3, 0)
+    for d, h, k in ((1, 0, 2), (1, 1, 3), (3, 1, 1), (2, 1, 5), (2, 0, 4)):
+        got_2(d, h, k)
+        to_core(d, h)
 
     direct = jnp.zeros((hidden.shape[0], SLOTS), F32)
-    for k in range(2):
+    down_stores = []
+    for turn in range(2):
+        k = core if turn == 0 else 1 - core
+        if turn == 1:
+            for d in (0, 3, 1, 2):
+                for h in range(2):
+                    from_y, from_x = lax.rem(y + 4 - d, 4), at_x(4 - d)
+                    links.got(along_y(k, from_y, h), k_core + 4 * d + h)
+                    links.got(along_x(k, from_x, h), k_core + 4 * d + 2 + h)
         for f in range(4):
-            at = pl.ds((2 * f + k) * FSL, FSL)
+            at = pl.ds(pl.multiple_of((2 * f + k) * FSL, FSL), FSL)
             part = jnp.concatenate([rows[k, (f - n) % 4, n].reshape(2 * HALF, FSL) for n in range(Y)], axis=0)
             direct += nt(w_s[:, at], part)
             down_ref[:, at] = mm(hidden_scaled, part).astype(BF16)
+            down_stores.append(load(down_ref.at[:, at], down_hbm.at[:, at], 21 + 4 * turn + f))
     slot_ref[...] = (direct * scale).astype(BF16)
     tot[0] = jnp.sum(hidden.astype(F32) * direct, axis=0, keepdims=True)
 
@@ -446,12 +494,11 @@
     outpg_ref[...] = iop_all[2:4].reshape(NS, 128)
 
     idx0, idx1 = jnp.broadcast_to(info[:, 0:1], (BLK, 128)), jnp.broadcast_to(info[:, 1:2], (BLK, 128))
-    rows8 = iota((BLK, 128), 0)
     pos0, pos1 = jnp.zeros((BLK, 128), F32), jnp.zeros((BLK, 128), F32)
     for i in range(BLK):
         i0, i1 = idx0[i : i + 1], idx1[i : i + 1]
-        pos0 += jnp.where((rows8 > i) & ((i0 == idx0) | (i1 == idx0)), 1.0, 0.0)
-        pos1 += jnp.where((rows8 > i) & ((i0 == idx1) | (i1 == idx1)), 1.0, 0.0)
+        pos0 += jnp.where((row8 > i) & ((i0 == idx0) | (i1 == idx0)), 1.0, 0.0)
+        pos1 += jnp.where((row8 > i) & ((i0 == idx1) | (i1 == idx1)), 1.0, 0.0)
     lane384 = iota((BLK, SLOTS), 1).astype(F32)
     base = ((c * Z + e) * CAP).astype(F32)
 
@@ -480,13 +527,33 @@
         val1 = jnp.where(info[:, 1:2] == expert, line, val1)
     out0 = jnp.sum(jnp.where(lane384 == base + pos0[:, 0:1], val0, 0.0), axis=1, keepdims=True)
     out1 = jnp.sum(jnp.where(lane384 == base + pos1[:, 0:1], val1, 0.0), axis=1, keepdims=True)
-    probg_ref[...] = jnp.where(iota((BLK, 2), 1) == 0, out0, out1)
+    diagonal = row8 == lane8
+    probg_ref[0:1, :] = jnp.sum(jnp.where(diagonal, out0, 0.0), axis=0, keepdims=True)[:, 0:BLK]
+    probg_ref[1:2, :] = jnp.sum(jnp.where(diagonal, out1, 0.0), axis=0, keepdims=True)[:, 0:BLK]
 
     @pl.when(t != 0)
     def _():
         pltpu.make_async_copy(wmix_ref, wbuf.at[0], local_sems.at[1]).wait()
 
+    for copy in down_stores:
+        copy.wait()
     links.drain()
+
+
+def store(*refs):
+    ins, outs, held, sems = refs[:9], refs[9:18], refs[18:27], refs[27]
+    steps = list(zip(ins, held, outs))
+    big = steps.pop(7)
+    steps += [[ref.at[pl.ds(n * 32, 32)] for ref in big] for n in range(7)]
+    loads = [pltpu.make_async_copy(src, mid, sems.at[0, n]) for n, (src, mid, _) in enumerate(steps)]
+    stores = [pltpu.make_async_copy(mid, dst, sems.at[1, n]) for n, (_, mid, dst) in enumerate(steps)]
+    for copy in loads:
+        copy.start()
+    for load, save in zip(loads, stores):
+        load.wait()
+        save.start()
+    for copy in stores:
+        copy.wait()
 
 
 def shards(
@@ -497,7 +564,7 @@
     features = down_weight.shape[2]
     vmem = pl.BlockSpec(memory_space=pltpu.VMEM)
     anywhere = pl.BlockSpec(memory_space=pl.ANY)
-    smem = pl.BlockSpec(memory_space=pltpu.SMEM)
+    hbm = pl.BlockSpec(memory_space=pltpu.HBM)
     shape = jax.ShapeDtypeStruct
     out = pl.pallas_call(
         body,
@@ -510,11 +577,24 @@
             shape((1, CH), F32),
             shape((hidden, SLOTS), BF16),
             shape((hidden, features), BF16),
-            shape((BLK, 2), F32),
+            shape((2, BLK), F32),
         ),
-        in_specs=[vmem, vmem, vmem, vmem, vmem, vmem, smem, vmem, anywhere, vmem, vmem, vmem, vmem, anywhere],
-        out_specs=tuple([vmem] * 9),
+        in_specs=[hbm] * 14,
+        out_specs=(vmem,) * 7 + (hbm, vmem),
         scratch_shapes=[
+            pltpu.VMEM((TOK, CH), BF16),
+            pltpu.VMEM((TOK, CH), F32),
+            pltpu.VMEM((NS, CH), F32),
+            pltpu.VMEM((NS, TOK), F32),
+            pltpu.VMEM((NS, TOK), F32),
+            pltpu.VMEM((1, CH), F32),
+            pltpu.SMEM((TOK,), jnp.int32),
+            pltpu.VMEM((TOK, CH), BF16),
+            pltpu.VMEM((BLK, features), BF16),
+            pltpu.SMEM((2, BLK), jnp.int32),
+            pltpu.SMEM((2, BLK), F32),
+            pltpu.VMEM((hidden, SLOTS), BF16),
+            pltpu.VMEM((hidden, features), BF16),
             pltpu.VMEM((TOK, CH), F32),
             pltpu.VMEM((TOK, CH), F32),
             pltpu.VMEM((TOK, NS, CH), F32),
@@ -552,19 +632,27 @@
             pltpu.VMEM((Z, 1, SLOTS), F32),
             pltpu.SemaphoreType.DMA((NSEM,)),
             pltpu.SemaphoreType.DMA((NSEM,)),
-            pltpu.SemaphoreType.DMA((2,)),
+            pltpu.SemaphoreType.DMA((32,)),
             pltpu.SemaphoreType.DMA((4,)),
         ],
         compiler_params=pltpu.CompilerParams(
-            collective_id=0, has_side_effects=True, vmem_limit_bytes=48 * 1024 * 1024
+            collective_id=0, has_side_effects=True, vmem_limit_bytes=VMEM_LIMIT
         ),
         name="scan_and_experts",
     )(
         mixer_input, step_sizes, decay_rates, input_proj, output_proj, skip_gain.reshape(1, CH), doc_starts, ssm_grad,
-        mixer_in_weight, residual_grad, expert_index_pairs, route_probs, hidden_saved[0], down_weight[0],
+        mixer_in_weight, residual_grad, expert_index_pairs.T, route_probs.T, hidden_saved[0], down_weight[0],
     )
-    ssm, stepg, inpg, outpg, decg, skipg, slot, down, probg = out
-    return ssm, stepg, inpg, outpg, decg, skipg.reshape(CH), slot[None], down[None], probg
+    ssm, stepg, inpg, outpg, decg, skipg, slot, down, probg = pl.pallas_call(
+        store,
+        out_shape=tuple(shape(array.shape, array.dtype) for array in out),
+        in_specs=[anywhere] * 9,
+        out_specs=tuple([hbm] * 9),
+        scratch_shapes=[pltpu.VMEM(array.shape, array.dtype) for array in out] + [pltpu.SemaphoreType.DMA((2, 16))],
+        compiler_params=pltpu.CompilerParams(vmem_limit_bytes=VMEM_LIMIT),
+        name="store_results",
+    )(*out)
+    return ssm, stepg, inpg, outpg, decg, skipg.reshape(CH), slot[None], down[None], probg.T
 
 
 def solution(mesh):

time: 122 us -> 103 us (0.84)
  local copies, waits for them, and re-layouts: 17.5 us -> 0 us
    unnamed x35 -> x0, local copies, waits for them, and re-layouts: 17.5 us -> none
    pallas_call x1, Pallas kernels: 103 us -> 99.6 us  [shards(): pl.pallas_call(body, out_shape=(shape((TOK, CH), BF16), shape((TOK, CH),...]
    pallas_call x0 -> x1, Pallas kernels: none -> 2.66 us  [shards(): pl.pallas_call(store, out_shape=tuple((shape(array.shape, array.dtype) fo...]
where the time goes in v2:
time: 103 us
  Pallas kernels  102 us (99%)
    pallas_call x1, Pallas kernels, shards(): pl.pallas_call(body, out_shape=(shape((TOK, CH), BF16), shape((TOK, CH),...  99.6 us
    pallas_call x1, Pallas kernels, shards(): pl.pallas_call(store, out_shape=tuple((shape(array.shape, array.dtype) fo...  2.66 us

profile of v2, /device:TPU:1, one launch (start us, length us, event | category | flops | bytes accessed | tf_op | source)
XLA Modules:
  0.0 102.9 jit_solution(14816961762229820829)
XLA Ops:
  0.6 99.6 %scan_and_experts.1 = (bf16[128,128]{1,0:T(8,128)(2,1)}, f32[128,128]{1,0:T(8,128)}, f32[16,128]{1,0:T(8,128)}, f32[16,128]{1,0:T(8,128)}, f32[16,128]{1,0:T(8,1...) custom-call(bf16[128,128]{1,0:T(8,128)(2,1)} %x_hbm.1, ...), custom_call_target="tpu_custom_call" | custom-call | tf_op jit(solution)/shard_map/scan_and_experts/pallas_call | solution.py:569
  100.3 2.7 %store_results.1 = (bf16[128,128]{1,0:T(8,128)(2,1)}, f32[128,128]{1,0:T(8,128)}, f32[16,128]{1,0:T(8,128)}, f32[16,128]{1,0:T(8,128)}, f32[16,128]{1,0:T(8,128)...) custom-call(bf16[128,128]{1,0:T(8,128)(2,1)} %get-tuple-element.27.refs_0_, ...), custom_call_target="tpu_custom_call" | custom-call | tf_op jit(solution)/shard_map/store_results/pallas_call | solution.py:646

commit v3 on v2

--- a/solution.py
+++ b/solution.py
@@ -71,18 +71,20 @@
         self.started = []
 
 
-NSEM = 160
+NSEM = 192
 VMEM_LIMIT = 60 * 1024 * 1024
 
 
 def body(
     x_hbm, step_hbm, rates_hbm, inp_hbm, outp_hbm, skip_hbm, doc_hbm, g_hbm, wmix_ref, resid_hbm,
     idx_hbm, prob_hbm, hidden_hbm, weight_ref,
-    ssm_ref, stepg_ref, inpg_ref, outpg_ref, decg_ref, skipg_ref, slot_ref, down_hbm, probg_ref,
+    ssm_hbm, stepg_hbm, inpg_hbm, outpg_hbm, decg_hbm, skipg_hbm, slot_hbm, down_hbm, probg_hbm,
     x_ref, step_ref, rates_ref, inp_ref, outp_ref, skip_ref, doc_ref, g_ref, resid_ref, idx_ref, prob_ref, hidden_ref, down_ref,
+    stepg_ref, inpg_ref, outpg_ref, decg_ref, skipg_ref, slot_ref, probg_ref,
+    gs, g0, g1x, g1y, a1, b1, g2a, g2b,
     xf, gf, a_s, inf_s, adj_s, ap_s, bsel, ssm_f, xbuf, sbuf, wbuf, pbuf, rbuf1, abuf, rbuf2,
     gbuf, ibuf, pair_out, pair_in, sel_s, scale_s, scale_in, rows, w_s,
-    iop, iop_in, iop_far, iop_near, iop_all, dsp, dsp_in, tot, tot_x, tot_c, tot_z,
+    iop, iop_in, iop_far, iop_near, iop_all, dsp, dsp_in, tot_p, tot_z,
     send_sems, recv_sems, local_sems, weight_sem,
 ):
     links = Links(send_sems, recv_sems)
@@ -185,6 +187,15 @@
     xbuf[0, 0:NS] = damp
     xbuf[0, NS : 2 * NS] = state
     xbuf[0, 2 * NS :] = back
+    for copy in late_loads:
+        copy.wait()
+    hidden_t = hidden_ref[...].T
+    for k in range(2):
+        for f in range(4):
+            part = mm(hidden_t, w_s[:, pl.ds((2 * f + k) * FSL, FSL)]).astype(BF16).reshape(Y, 2, HALF, FSL)
+            for n in range(Y):
+                gs[k, (f - n) % 4, n] = part[n]
+
     pl.semaphore_wait(barrier, partners)
     k_ctx = links.slot(CTX)
     for dc in range(1, CTX):
@@ -213,6 +224,13 @@
             links.n_send += 1
             copy.start()
             links.started.append(copy)
+
+    other_core = 2 * y + (1 - core)
+    k_g0 = links.slot(8)
+    for n in range(X):
+        for h in range(2):
+            half = pl.ds(2 * h, 2)
+            links.put(gs.at[1 - core, n, half], g0.at[n, half], k_g0 + 2 * n + h, ctx=other_core)
 
     links.got(pair_in, k_pair)
     mine = info
@@ -283,9 +301,8 @@
     acc_in, acc_out, acc_decay = lax.fori_loop(0, NBLK, gradients, (zero, zero, zero))
 
     ssm_bf = ssm_f[...].astype(BF16)
-    ssm_ref[...] = ssm_bf
     sbuf[0, 0] = ssm_bf
-    other_core = 2 * y + (1 - core)
+    stores = [load(sbuf.at[0, 0], ssm_hbm, 29), load(stepg_ref, stepg_hbm, 30)]
     k_s = links.slot(2 * X)
     for dx in (2, 1, 3):
         links.put(sbuf.at[0, 0], sbuf.at[0, dx], k_s + dx, tp=at_x(dx))
@@ -328,6 +345,11 @@
     for dy in range(1, 4):
         links.put(scale_s.at[0], scale_in.at[dy], k_scale + dy, ctx=at_y(dy))
 
+    for n in range(X):
+        for h in range(2):
+            links.got(g0.at[n, pl.ds(2 * h, 2)], k_g0 + 2 * n + h)
+        gs[core, n] = (gs[core, n].astype(F32) + g0[n].astype(F32)).astype(BF16)
+
     for n in range(4):
         pltpu.make_async_copy(wbuf.at[n], wbuf.at[n], weight_sem.at[n]).wait()
     for dx in (1, 3, 2):
@@ -335,6 +357,10 @@
         links.put(sbuf.at[0, dx], sbuf.at[1, dx], k_s + X + dx, ctx=other_core)
     for dx in (0, 1, 3, 2):
         links.got(sbuf.at[1, dx], k_s + X + dx)
+    k_g1 = links.slot(8)
+    for d in (2, 1, 3):
+        links.put(gs.at[core, at_x(d), :, 0], g1x.at[d], k_g1 + d, tp=at_x(d))
+        links.put(gs.at[core, :, lax.rem(y + d, 4), 1], g1y.at[d], k_g1 + 4 + d, ctx=at_y(d))
     mixer = wbuf[...].reshape(4 * 128, FSL)
     parts = []
     for k in range(2):
@@ -375,22 +401,43 @@
         total += rbuf2[n].astype(F32)
 
     gbuf[r0, q0] = total.astype(BF16)
-    k_g1 = links.slot(3)
+    k_a1 = links.slot(3)
     for n, dz in enumerate(FAR):
-        links.put(gbuf.at[r0, q0], gbuf.at[r0, q0], k_g1 + n, exp=at_z(dz))
+        links.put(gbuf.at[r0, q0], gbuf.at[r0, q0], k_a1 + n, exp=at_z(dz))
+    for d in (1, 3, 2):
+        links.got(g1x.at[d], k_g1 + d)
+        links.got(g1y.at[d], k_g1 + 4 + d)
+    for n in range(4):
+        over_x, over_y = gs[core, t, n, 0].astype(F32), gs[core, n, y, 1].astype(F32)
+        for d in range(1, 4):
+            over_x += g1x[d, n].astype(F32)
+            over_y += g1y[d, n].astype(F32)
+        a1[n] = over_x.astype(BF16)
+        b1[n] = over_y.astype(BF16)
+    k_g2 = links.slot(8)
+    for d in (2, 1, 3):
+        links.put(a1.at[lax.rem(y + d, 4)], g2a.at[d], k_g2 + d, ctx=at_y(d))
+        links.put(b1.at[at_x(d)], g2b.at[d], k_g2 + 4 + d, tp=at_x(d))
     for n in range(3):
         links.got(iop_far.at[n + 1], k_iof + n)
     iop_near[0] = iop_far[0] + iop_far[1] + iop_far[2] + iop_far[3]
     for n, dz in enumerate(FAR):
-        links.got(gbuf.at[r0, lax.rem(q0 + 4 - dz // 4, 4)], k_g1 + n)
-    k_g2 = links.slot(3)
+        links.got(gbuf.at[r0, lax.rem(q0 + 4 - dz // 4, 4)], k_a1 + n)
+    k_a2 = links.slot(3)
     for n, dz in enumerate(near):
-        links.put(gbuf.at[r0], gbuf.at[r0], k_g2 + n, exp=at_z(dz))
+        links.put(gbuf.at[r0], gbuf.at[r0], k_a2 + n, exp=at_z(dz))
     k_ion = links.slot(4)
     for n, dz in enumerate(near):
         links.put(iop_near.at[0], iop_near.at[n + 1], k_ion + n, exp=at_z(dz))
+    for d in (1, 3, 2):
+        links.got(g2a.at[d], k_g2 + d)
+        links.got(g2b.at[d], k_g2 + 4 + d)
+    weight_low, weight_high = a1[y].astype(F32), b1[t].astype(F32)
+    for d in range(1, 4):
+        weight_low += g2a[d].astype(F32)
+        weight_high += g2b[d].astype(F32)
     for n, dz in enumerate(near):
-        links.got(gbuf.at[lax.rem(r0 + 16 - dz, 4)], k_g2 + n)
+        links.got(gbuf.at[lax.rem(r0 + 16 - dz, 4)], k_a2 + n)
 
     picked_rows = mm(sel_s[...], gbuf[...].reshape(256, FSL)).astype(BF16)
     rows[core, t, y, 0] = picked_rows[0:HALF]
@@ -399,6 +446,26 @@
     for d in (2, 1, 3):
         links.put(rows.at[core, t, y, 0], rows.at[core, t, y, 0], k_p1 + d, tp=at_x(d))
         links.put(rows.at[core, t, y, 1], rows.at[core, t, y, 1], k_p1 + 4 + d, ctx=at_y(d))
+    product = jnp.concatenate(
+        [
+            picked_rows[0:HALF].astype(F32) * weight_low,
+            picked_rows[HALF : 2 * HALF].astype(F32) * weight_high,
+            jnp.zeros((128 - 2 * HALF, FSL), F32),
+        ],
+        axis=0,
+    )
+    high = product.astype(BF16)
+    low = (product - high.astype(F32)).astype(BF16)
+    ones = jnp.ones((BLK, FSL), BF16)
+    tot_p[0] = nt(ones, high) + nt(ones, low)
+    k_tp = links.slot(2 * X)
+    for dk in range(2):
+        for dx in range(X):
+            if dk or dx:
+                links.put(
+                    tot_p.at[0], tot_p.at[dk * X + dx], k_tp + dk * X + dx,
+                    ctx=2 * y + lax.rem(core + dk, 2), tp=at_x(dx),
+                )
     for d in (1, 3, 2):
         links.got(rows.at[core, at_x(4 - d), y, 0], k_p1 + d)
         links.got(rows.at[core, t, lax.rem(y + 4 - d, 4), 1], k_p1 + 4 + d)
@@ -428,6 +495,15 @@
 
     to_core(0, 0)
     to_core(0, 1)
+    for n in range(1, 2 * X):
+        links.got(tot_p.at[n], k_tp + n)
+    slot_total = tot_p[0]
+    for n in range(1, 2 * X):
+        slot_total += tot_p[n]
+    tot_z[0] = slot_total
+    k_tz = links.slot(Z)
+    for dz in range(1, Z):
+        links.put(tot_z.at[0], tot_z.at[dz], k_tz + dz, exp=at_z(dz))
 
     for n in range(3):
         links.got(iop_near.at[n + 1], k_ion + n)
@@ -443,16 +519,13 @@
         sums += dsp_in[dc]
     decg_ref[...] = sums[0:NS]
     skipg_ref[...] = sums[NS : NS + 1]
+    stores += [load(decg_ref, decg_hbm, 31), load(skipg_ref, skipg_hbm, 32)]
     for dy in range(1, 4):
         links.got(scale_in.at[dy], k_scale + dy)
     scale = scale_s[0] + scale_in[1] + scale_in[2] + scale_in[3]
 
-    late_loads[0].wait()
     hidden = hidden_ref[...]
     hidden_scaled = (hidden.astype(F32) * scale).astype(BF16)
-    for copy in late_loads[1:]:
-        copy.wait()
-
     def got_2(d, h, k):
         links.got(along_y(core, lax.rem(y + 4 - d, 4), h), k_p2 + k)
         links.got(along_x(core, at_x(4 - d), h), k_p2 + 6 + k)
@@ -482,16 +555,14 @@
             down_ref[:, at] = mm(hidden_scaled, part).astype(BF16)
             down_stores.append(load(down_ref.at[:, at], down_hbm.at[:, at], 21 + 4 * turn + f))
     slot_ref[...] = (direct * scale).astype(BF16)
-    tot[0] = jnp.sum(hidden.astype(F32) * direct, axis=0, keepdims=True)
-
-    k_tx = links.slot(4)
-    for dx in range(1, X):
-        links.put(tot.at[0], tot_x.at[dx], k_tx + dx, tp=at_x(dx))
+    stores.append(load(slot_ref, slot_hbm, 33))
+
     for dx in range(1, X):
         links.got(iop_all.at[at_x(4 - dx)], k_ioa + dx)
     iop_all[t] = iop_out
     inpg_ref[...] = iop_all[0:2].reshape(NS, 128)
     outpg_ref[...] = iop_all[2:4].reshape(NS, 128)
+    stores += [load(inpg_ref, inpg_hbm, 34), load(outpg_ref, outpg_hbm, 35)]
 
     idx0, idx1 = jnp.broadcast_to(info[:, 0:1], (BLK, 128)), jnp.broadcast_to(info[:, 1:2], (BLK, 128))
     pos0, pos1 = jnp.zeros((BLK, 128), F32), jnp.zeros((BLK, 128), F32)
@@ -499,43 +570,26 @@
         i0, i1 = idx0[i : i + 1], idx1[i : i + 1]
         pos0 += jnp.where((row8 > i) & ((i0 == idx0) | (i1 == idx0)), 1.0, 0.0)
         pos1 += jnp.where((row8 > i) & ((i0 == idx1) | (i1 == idx1)), 1.0, 0.0)
-    lane384 = iota((BLK, SLOTS), 1).astype(F32)
-    base = ((c * Z + e) * CAP).astype(F32)
-
-    for dx in range(1, X):
-        links.got(tot_x.at[dx], k_tx + dx)
-    tot_c[0] = tot[0] + tot_x[1] + tot_x[2] + tot_x[3]
-    k_tc = links.slot(CTX)
-    for dc in range(1, CTX):
-        links.put(tot_c.at[0], tot_c.at[dc], k_tc + dc, ctx=lax.rem(c + dc, CTX))
-    for dc in range(1, CTX):
-        links.got(tot_c.at[dc], k_tc + dc)
-    plane = tot_c[0]
-    for dc in range(1, CTX):
-        plane += tot_c[dc]
-    tot_z[0] = plane
-    k_tz = links.slot(Z)
-    for dz in range(1, Z):
-        links.put(tot_z.at[0], tot_z.at[dz], k_tz + dz, exp=at_z(dz))
+    own_lane = lane8.astype(F32) - ((core * Z + e) * CAP).astype(F32)
     for dz in range(1, Z):
         links.got(tot_z.at[dz], k_tz + dz)
-    val0, val1 = jnp.zeros((BLK, SLOTS), F32), jnp.zeros((BLK, SLOTS), F32)
+    val0, val1 = jnp.zeros((BLK, 128), F32), jnp.zeros((BLK, 128), F32)
     for dz in range(Z):
         expert = at_z(Z - dz).astype(F32)
-        line = jnp.broadcast_to(tot_z[dz], (BLK, SLOTS))
-        val0 = jnp.where(info[:, 0:1] == expert, line, val0)
-        val1 = jnp.where(info[:, 1:2] == expert, line, val1)
-    out0 = jnp.sum(jnp.where(lane384 == base + pos0[:, 0:1], val0, 0.0), axis=1, keepdims=True)
-    out1 = jnp.sum(jnp.where(lane384 == base + pos1[:, 0:1], val1, 0.0), axis=1, keepdims=True)
+        val0 = jnp.where(idx0 == expert, tot_z[dz], val0)
+        val1 = jnp.where(idx1 == expert, tot_z[dz], val1)
+    out0 = jnp.sum(jnp.where(own_lane == pos0, val0, 0.0), axis=1, keepdims=True)
+    out1 = jnp.sum(jnp.where(own_lane == pos1, val1, 0.0), axis=1, keepdims=True)
     diagonal = row8 == lane8
     probg_ref[0:1, :] = jnp.sum(jnp.where(diagonal, out0, 0.0), axis=0, keepdims=True)[:, 0:BLK]
     probg_ref[1:2, :] = jnp.sum(jnp.where(diagonal, out1, 0.0), axis=0, keepdims=True)[:, 0:BLK]
+    stores.append(load(probg_ref, probg_hbm, 36))
 
     @pl.when(t != 0)
     def _():
         pltpu.make_async_copy(wmix_ref, wbuf.at[0], local_sems.at[1]).wait()
 
-    for copy in down_stores:
+    for copy in stores + down_stores:
         copy.wait()
     links.drain()
 
@@ -562,7 +616,6 @@
 ):
     hidden = hidden_saved[0].shape[0]
     features = down_weight.shape[2]
-    vmem = pl.BlockSpec(memory_space=pltpu.VMEM)
     anywhere = pl.BlockSpec(memory_space=pl.ANY)
     hbm = pl.BlockSpec(memory_space=pltpu.HBM)
     shape = jax.ShapeDtypeStruct
@@ -580,7 +633,7 @@
             shape((2, BLK), F32),
         ),
         in_specs=[hbm] * 14,
-        out_specs=(vmem,) * 7 + (hbm, vmem),
+        out_specs=(hbm,) * 9,
         scratch_shapes=[
             pltpu.VMEM((TOK, CH), BF16),
             pltpu.VMEM((TOK, CH), F32),
@@ -595,6 +648,21 @@
             pltpu.SMEM((2, BLK), F32),
             pltpu.VMEM((hidden, SLOTS), BF16),
             pltpu.VMEM((hidden, features), BF16),
+            pltpu.VMEM((TOK, CH), F32),
+            pltpu.VMEM((NS, TOK), F32),
+            pltpu.VMEM((NS, TOK), F32),
+            pltpu.VMEM((NS, CH), F32),
+            pltpu.VMEM((1, CH), F32),
+            pltpu.VMEM((hidden, SLOTS), BF16),
+            pltpu.VMEM((2, BLK), F32),
+            pltpu.VMEM((2, X, Y, 2, HALF, FSL), BF16),
+            pltpu.VMEM((X, Y, 2, HALF, FSL), BF16),
+            pltpu.VMEM((4, Y, HALF, FSL), BF16),
+            pltpu.VMEM((4, X, HALF, FSL), BF16),
+            pltpu.VMEM((Y, HALF, FSL), BF16),
+            pltpu.VMEM((X, HALF, FSL), BF16),
+            pltpu.VMEM((4, HALF, FSL), BF16),
+            pltpu.VMEM((4, HALF, FSL), BF16),
             pltpu.VMEM((TOK, CH), F32),
             pltpu.VMEM((TOK, CH), F32),
             pltpu.VMEM((TOK, NS, CH), F32),
@@ -626,13 +694,11 @@
             pltpu.VMEM((4, 8, 128), F32),
             pltpu.VMEM((NS + BLK, CH), F32),
             pltpu.VMEM((CTX, NS + BLK, CH), F32),
-            pltpu.VMEM((1, 1, SLOTS), F32),
-            pltpu.VMEM((4, 1, SLOTS), F32),
-            pltpu.VMEM((CTX, 1, SLOTS), F32),
-            pltpu.VMEM((Z, 1, SLOTS), F32),
+            pltpu.VMEM((2 * X, BLK, 128), F32),
+            pltpu.VMEM((Z, BLK, 128), F32),
             pltpu.SemaphoreType.DMA((NSEM,)),
             pltpu.SemaphoreType.DMA((NSEM,)),
-            pltpu.SemaphoreType.DMA((32,)),
+            pltpu.SemaphoreType.DMA((40,)),
             pltpu.SemaphoreType.DMA((4,)),
         ],
         compiler_params=pltpu.CompilerParams(

time: 103 us -> 88.6 us (0.86)
  Pallas kernels: 102 us -> 87 us
    pallas_call x1, Pallas kernels: 99.6 us -> 84.3 us  [shards(): pl.pallas_call(body, out_shape=(shape((TOK, CH), BF16), shape((TOK, CH),...]
where the time goes in v3:
time: 88.6 us; the launch traced here: 87.6 us
  Pallas kernels  87 us (98%)
    pallas_call x1, Pallas kernels, shards(): pl.pallas_call(body, out_shape=(shape((TOK, CH), BF16), shape((TOK, CH),...  84.3 us
    pallas_call x1, Pallas kernels, shards(): pl.pallas_call(store, out_shape=tuple((shape(array.shape, array.dtype) fo...  2.66 us

profile of v3, /device:TPU:1, one launch (start us, length us, event | category | flops | bytes accessed | tf_op | source)
XLA Modules:
  0.0 87.6 jit_solution(14135603952813045918)
XLA Ops:
  0.6 84.3 %scan_and_experts.1 = (bf16[128,128]{1,0:T(8,128)(2,1)}, f32[128,128]{1,0:T(8,128)}, f32[16,128]{1,0:T(8,128)}, f32[16,128]{1,0:T(8,128)}, f32[16,128]{1,0:T(8,1...) custom-call(bf16[128,128]{1,0:T(8,128)(2,1)} %x_hbm.1, ...), custom_call_target="tpu_custom_call" | custom-call | tf_op jit(solution)/shard_map/scan_and_experts/pallas_call | solution.py:622
  85.0 2.7 %store_results.1 = (bf16[128,128]{1,0:T(8,128)(2,1)}, f32[128,128]{1,0:T(8,128)}, f32[16,128]{1,0:T(8,128)}, f32[16,128]{1,0:T(8,128)}, f32[16,128]{1,0:T(8,128)...) custom-call(bf16[128,128]{1,0:T(8,128)(2,1)} %get-tuple-element.27.refs_0_, ...), custom_call_target="tpu_custom_call" | custom-call | tf_op jit(solution)/shard_map/store_results/pallas_call | solution.py:712

commit v4 on v3

--- a/solution.py
+++ b/solution.py
@@ -20,7 +20,7 @@
 CAP = 3
 HALF = Z * CAP
 SLOTS = CTX * HALF
-FAR = (4, 12, 8)
+FAR = (10, 14, 2, 6)
 
 
 def nt(a, b):
@@ -71,7 +71,7 @@
         self.started = []
 
 
-NSEM = 192
+NSEM = 256
 VMEM_LIMIT = 60 * 1024 * 1024
 
 
@@ -83,15 +83,14 @@
     stepg_ref, inpg_ref, outpg_ref, decg_ref, skipg_ref, slot_ref, probg_ref,
     gs, g0, g1x, g1y, a1, b1, g2a, g2b,
     xf, gf, a_s, inf_s, adj_s, ap_s, bsel, ssm_f, xbuf, sbuf, wbuf, pbuf, rbuf1, abuf, rbuf2,
-    gbuf, ibuf, pair_out, pair_in, sel_s, scale_s, scale_in, rows, w_s,
+    gbuf, ibuf, gown, iown, pair_out, pair_in, sel_s, scale_s, scale_in, rows, w_s,
     iop, iop_in, iop_far, iop_near, iop_all, dsp, dsp_in, tot_p, tot_z,
     send_sems, recv_sems, local_sems, weight_sem,
 ):
     links = Links(send_sems, recv_sems)
     c, e, t = lax.axis_index("ctx"), lax.axis_index("exp"), lax.axis_index("tp")
     y, core = lax.div(c, 2), lax.rem(c, 2)
-    r0, q0 = lax.rem(e, 4), lax.div(e, 4)
-    fs = 2 * lax.rem(t + y, 4) + core
+    fs = 2 * lax.rem(t + y + 2 * core, 4) + core
 
     def at_y(dy):
         return 2 * lax.rem(y + dy, 4) + core
@@ -144,7 +143,7 @@
             info = jnp.where((row8 == i) & (lane8 == k), idx_ref[k, i].astype(F32), info)
             info = jnp.where((row8 == i) & (lane8 == 2 + k), prob_ref[k, i], info)
     info = info.astype(BF16).astype(F32)
-    other_fs = 2 * lax.rem(t + y, 4) + (1 - core)
+    other_fs = 2 * lax.rem(t + y + 2 * (1 - core), 4) + (1 - core)
     pair_out[:, 0:FSL] = resid_ref[:, pl.ds(pl.multiple_of(other_fs * FSL, FSL), FSL)].astype(F32)
     pair_out[:, FSL:] = info
     xf[...] = x_ref[...].astype(F32)
@@ -194,7 +193,7 @@
         for f in range(4):
             part = mm(hidden_t, w_s[:, pl.ds((2 * f + k) * FSL, FSL)]).astype(BF16).reshape(Y, 2, HALF, FSL)
             for n in range(Y):
-                gs[k, (f - n) % 4, n] = part[n]
+                gs[k, (f - n - 2 * k) % 4, n] = part[n]
 
     pl.semaphore_wait(barrier, partners)
     k_ctx = links.slot(CTX)
@@ -204,22 +203,24 @@
     k_pair = links.slot()
     links.put(pair_out, pair_in, k_pair, ctx=2 * y + (1 - core))
 
-    for dy in range(4):
-        if dy == 0:
-            @pl.when(t == 0)
+    for turn in range(4):
+        dy = lax.rem(t + 2 * core + turn, 4)
+        target = {"ctx": at_y(dy), "tp": lax.rem(8 - dy + 2 * core, 4)}
+        if turn == 0:
+            @pl.when(t == 2 * core)
             def _():
-                pltpu.make_async_copy(wmix_ref, wbuf.at[0], weight_sem.at[0]).start()
-
-            @pl.when(t != 0)
+                pltpu.make_async_copy(wmix_ref, wbuf.at[t], weight_sem.at[t]).start()
+
+            @pl.when(t != 2 * core)
             def _():
                 pltpu.make_async_remote_copy(
                     src_ref=wmix_ref, dst_ref=wbuf.at[t], send_sem=local_sems.at[1], recv_sem=weight_sem.at[t],
-                    device_id={"tp": 0}, device_id_type=MESH,
+                    device_id=target, device_id_type=MESH,
                 ).start()
         else:
             copy = pltpu.make_async_remote_copy(
                 src_ref=wmix_ref, dst_ref=wbuf.at[t], send_sem=send_sems.at[links.n_send],
-                recv_sem=weight_sem.at[t], device_id={"ctx": at_y(dy), "tp": (4 - dy) % 4}, device_id_type=MESH,
+                recv_sem=weight_sem.at[t], device_id=target, device_id_type=MESH,
             )
             links.n_send += 1
             copy.start()
@@ -236,11 +237,11 @@
     mine = info
     theirs = pair_in[:, FSL:]
     first = core == 0
-    ibuf[r0, q0, 0:BLK] = jnp.where(first, mine, theirs)
-    ibuf[r0, q0, BLK:] = jnp.where(first, theirs, mine)
-    k_ifar = links.slot(3)
+    iown[0:BLK] = jnp.where(first, mine, theirs)
+    iown[BLK:] = jnp.where(first, theirs, mine)
+    k_ifar = links.slot(4)
     for n, dz in enumerate(FAR):
-        links.put(ibuf.at[r0, q0], ibuf.at[r0, q0], k_ifar + n, exp=at_z(dz))
+        links.put(iown, ibuf.at[0, n], k_ifar + n, exp=at_z(dz))
 
     for dc in range(1, CTX):
         links.got(xbuf.at[dc], k_ctx + dc)
@@ -269,11 +270,11 @@
 
     lax.fori_loop(0, NBLK, scan, (entering, arriving))
 
-    for n, dz in enumerate(FAR):
-        links.got(ibuf.at[r0, lax.rem(q0 + 4 - dz // 4, 4)], k_ifar + n)
+    for n in range(4):
+        links.got(ibuf.at[0, n], k_ifar + n)
     k_inear = links.slot(3)
     for n, dz in enumerate(near):
-        links.put(ibuf.at[r0], ibuf.at[r0], k_inear + n, exp=at_z(dz))
+        links.put(ibuf.at[0], ibuf.at[1 + n], k_inear + n, exp=at_z(dz))
 
     rates = rates_ref[...]
     ones8 = jnp.where(iota((BLK, 128), 0) == lax.div(lane8, NS), 1.0, 0.0).astype(BF16)
@@ -320,8 +321,8 @@
     for dc in range(1, CTX):
         links.put(dsp, dsp_in.at[dc], k_dsp + dc, ctx=lax.rem(c + dc, CTX))
 
-    for n, dz in enumerate(near):
-        links.got(ibuf.at[lax.rem(r0 + 16 - dz, 4)], k_inear + n)
+    for n in range(3):
+        links.got(ibuf.at[1 + n], k_inear + n)
     infos = ibuf[...].reshape(256, 128)
     e_f = e.astype(F32)
     hit0 = jnp.where(infos[:, 0:1] == e_f, 1.0, 0.0)
@@ -332,9 +333,11 @@
     before = jnp.where((lax.div(r256, BLK) == lax.div(l256, BLK)) & (r256 > l256), 1.0, 0.0).astype(BF16)
     position = mm(before, hit.astype(BF16))
     tok_row = iota((256, 128), 0)
-    tok_r, tok_q = lax.div(tok_row, 64), lax.rem(lax.div(tok_row, 16), 4)
+    tok_near, tok_far = lax.div(tok_row, 64), lax.rem(lax.div(tok_row, 16), 4)
+    near_of = jnp.where(tok_near == 1, 1, jnp.where(tok_near == 2, 15, jnp.where(tok_near == 3, 2 + 12 * core, 0)))
+    tok_block = lax.rem(e + 4 * Z - near_of - 10 - 4 * tok_far, Z)
     tok_k = lax.rem(lax.div(tok_row, BLK), 2)
-    tok_slot = (tok_k * Z + tok_q * 4 + tok_r) * CAP
+    tok_slot = (tok_k * Z + tok_block) * CAP
     slot_of = tok_slot.astype(F32) + position
     picked = jnp.where(iota((256, 128), 1).astype(F32) == slot_of, hit, 0.0)
     sel_s[...] = picked.T.astype(BF16)
@@ -369,41 +372,42 @@
         parts.append(mm(lhs, mixer).reshape(Z, BLK, FSL))
     chunks = jnp.concatenate(parts, axis=1).astype(BF16)
     for n in range(Z):
-        pbuf[n % 4, n // 4] = chunks[n]
+        ahead = lax.rem(n + Z - e, Z)
+        pbuf[lax.rem(ahead, 4), lax.div(ahead, 4)] = chunks[n]
 
     k_r1 = links.slot(3)
     for n, dz in enumerate(near):
-        links.put(pbuf.at[lax.rem(r0 + dz, 4)], rbuf1.at[n], k_r1 + n, exp=at_z(dz))
+        links.put(pbuf.at[(3, 1, 0)[n]], rbuf1.at[n], k_r1 + n, exp=at_z(dz))
     for dx in range(1, X):
         links.got(iop_in.at[dx], k_iox + dx)
-    iop_far[0] = iop[t] + iop_in[1] + iop_in[2] + iop_in[3]
+    iop_far[4] = iop[t] + iop_in[1] + iop_in[2] + iop_in[3]
     k_iof = links.slot(4)
     for n, dz in enumerate(FAR):
-        links.put(iop_far.at[0], iop_far.at[n + 1], k_iof + n, exp=at_z(dz))
+        links.put(iop_far.at[4], iop_far.at[n], k_iof + n, exp=at_z(dz))
     for n in range(3):
         links.got(rbuf1.at[n], k_r1 + n)
-    summed = pbuf[r0].astype(F32)
-    for n in range(3):
-        summed += rbuf1[n].astype(F32)
-    abuf[...] = summed.astype(BF16)
-    k_r2 = links.slot(3)
-    for n, dz in enumerate(FAR):
-        links.put(abuf.at[lax.rem(q0 + dz // 4, 4)], rbuf2.at[n], k_r2 + n, exp=at_z(dz))
+    k_r2 = links.slot(4)
+    for n, dz in ((0, 10), (3, 6), (1, 14), (2, 2)):
+        at = (2 + n) % 4
+        summed = pbuf[2, at].astype(F32) + rbuf1[0, at].astype(F32) + rbuf1[1, at].astype(F32)
+        summed += rbuf1[2, lax.rem(3 - core + n, 4)].astype(F32)
+        abuf[n] = summed.astype(BF16)
+        links.put(abuf.at[n], rbuf2.at[n], k_r2 + n, exp=at_z(dz))
     own_resid = resid_ref[:, pl.ds(pl.multiple_of(fs * FSL, FSL), FSL)].astype(F32)
     their_resid = pair_in[:, 0:FSL]
     resid = jnp.concatenate(
         [jnp.where(first, own_resid, their_resid), jnp.where(first, their_resid, own_resid)], axis=0
     )
-    for n in range(3):
+    for n in range(4):
         links.got(rbuf2.at[n], k_r2 + n)
-    total = abuf[q0].astype(F32) + resid
-    for n in range(3):
+    total = resid
+    for n in range(4):
         total += rbuf2[n].astype(F32)
 
-    gbuf[r0, q0] = total.astype(BF16)
-    k_a1 = links.slot(3)
+    gown[...] = total.astype(BF16)
+    k_a1 = links.slot(4)
     for n, dz in enumerate(FAR):
-        links.put(gbuf.at[r0, q0], gbuf.at[r0, q0], k_a1 + n, exp=at_z(dz))
+        links.put(gown, gbuf.at[0, n], k_a1 + n, exp=at_z(dz))
     for d in (1, 3, 2):
         links.got(g1x.at[d], k_g1 + d)
         links.got(g1y.at[d], k_g1 + 4 + d)
@@ -418,14 +422,14 @@
     for d in (2, 1, 3):
         links.put(a1.at[lax.rem(y + d, 4)], g2a.at[d], k_g2 + d, ctx=at_y(d))
         links.put(b1.at[at_x(d)], g2b.at[d], k_g2 + 4 + d, tp=at_x(d))
-    for n in range(3):
-        links.got(iop_far.at[n + 1], k_iof + n)
+    for n in range(4):
+        links.got(iop_far.at[n], k_iof + n)
     iop_near[0] = iop_far[0] + iop_far[1] + iop_far[2] + iop_far[3]
-    for n, dz in enumerate(FAR):
-        links.got(gbuf.at[r0, lax.rem(q0 + 4 - dz // 4, 4)], k_a1 + n)
+    for n in range(4):
+        links.got(gbuf.at[0, n], k_a1 + n)
     k_a2 = links.slot(3)
     for n, dz in enumerate(near):
-        links.put(gbuf.at[r0], gbuf.at[r0], k_a2 + n, exp=at_z(dz))
+        links.put(gbuf.at[0], gbuf.at[1 + n], k_a2 + n, exp=at_z(dz))
     k_ion = links.slot(4)
     for n, dz in enumerate(near):
         links.put(iop_near.at[0], iop_near.at[n + 1], k_ion + n, exp=at_z(dz))
@@ -436,16 +440,55 @@
     for d in range(1, 4):
         weight_low += g2a[d].astype(F32)
         weight_high += g2b[d].astype(F32)
-    for n, dz in enumerate(near):
-        links.got(gbuf.at[lax.rem(r0 + 16 - dz, 4)], k_a2 + n)
+    for n in range(3):
+        links.got(gbuf.at[1 + n], k_a2 + n)
 
     picked_rows = mm(sel_s[...], gbuf[...].reshape(256, FSL)).astype(BF16)
     rows[core, t, y, 0] = picked_rows[0:HALF]
     rows[core, t, y, 1] = picked_rows[HALF : 2 * HALF]
-    k_p1 = links.slot(8)
+    def piece(axis, k, step, d=0):
+        if axis == 0:
+            return rows.at[k, at_x(step), lax.rem(y + 4 - d, 4), 0]
+        return rows.at[k, at_x(4 - d), lax.rem(y + step, 4), 1]
+
+    def pass_on(axis, step, d_from, slot, d):
+        device = {"ctx": at_y(d)} if axis == 0 else {"tp": at_x(d)}
+        links.put(piece(axis, core, step, d_from), piece(axis, core, step, d_from), slot, **device)
+
+    k_p1, k_p2, k_core = links.slot(8), links.slot(32), links.slot(32)
+
+    def slot_2(axis, step, d):
+        return k_p2 + 16 * axis + 4 * step + d
+
+    def to_core(axis, step, d):
+        ref = piece(axis, core, step, d)
+        links.put(ref, ref, k_core + 16 * axis + 4 * step + d, ctx=other_core)
+
+    def got_1(d):
+        for axis in range(2):
+            step = 4 - d
+            links.got(piece(axis, core, step), k_p1 + 4 * axis + d)
+            for to in ((1, 3, 2) if d == 2 else (3, 1)):
+                pass_on(axis, step, 0, slot_2(axis, step, to), to)
+        for axis in range(2):
+            to_core(axis, 4 - d, 0)
+
+    def got_2(step, d, relay=False):
+        for axis in range(2):
+            links.got(piece(axis, core, step, d), slot_2(axis, step, d))
+            if relay:
+                pass_on(axis, step, 3, slot_2(axis, step, 2), 3)
+        for axis in range(2):
+            to_core(axis, step, d)
+
     for d in (2, 1, 3):
         links.put(rows.at[core, t, y, 0], rows.at[core, t, y, 0], k_p1 + d, tp=at_x(d))
         links.put(rows.at[core, t, y, 1], rows.at[core, t, y, 1], k_p1 + 4 + d, ctx=at_y(d))
+    for d in (3, 1):
+        for axis in range(2):
+            pass_on(axis, 0, 0, slot_2(axis, 0, d), d)
+    for axis in range(2):
+        to_core(axis, 0, 0)
     product = jnp.concatenate(
         [
             picked_rows[0:HALF].astype(F32) * weight_low,
@@ -466,35 +509,10 @@
                     tot_p.at[0], tot_p.at[dk * X + dx], k_tp + dk * X + dx,
                     ctx=2 * y + lax.rem(core + dk, 2), tp=at_x(dx),
                 )
-    for d in (1, 3, 2):
-        links.got(rows.at[core, at_x(4 - d), y, 0], k_p1 + d)
-        links.got(rows.at[core, t, lax.rem(y + 4 - d, 4), 1], k_p1 + 4 + d)
-
-    def along_y(k, from_y, h):
-        return rows.at[k, pl.ds(2 * h, 2), from_y, 0]
-
-    def along_x(k, from_x, h):
-        return rows.at[k, from_x, pl.ds(2 * h, 2), 1]
-
-    def put_y(from_y, h, slot, dy):
-        links.put(along_y(core, from_y, h), along_y(core, from_y, h), slot, ctx=at_y(dy))
-
-    def put_x(from_x, h, slot, dx):
-        links.put(along_x(core, from_x, h), along_x(core, from_x, h), slot, tp=at_x(dx))
-
-    k_p2 = links.slot(12)
-    for d, h, k in ((3, 0, 0), (1, 0, 2), (1, 1, 3), (2, 1, 5), (3, 1, 1)):
-        put_y(y, h, k_p2 + k, d)
-        put_x(t, h, k_p2 + 6 + k, d)
-    k_core = links.slot(16)
-
-    def to_core(d, h):
-        from_y, from_x = lax.rem(y + 4 - d, 4), at_x(4 - d)
-        links.put(along_y(core, from_y, h), along_y(core, from_y, h), k_core + 4 * d + h, ctx=other_core)
-        links.put(along_x(core, from_x, h), along_x(core, from_x, h), k_core + 4 * d + 2 + h, ctx=other_core)
-
-    to_core(0, 0)
-    to_core(0, 1)
+    got_1(1)
+    got_1(3)
+    got_2(0, 3, relay=True)
+    got_1(2)
     for n in range(1, 2 * X):
         links.got(tot_p.at[n], k_tp + n)
     slot_total = tot_p[0]
@@ -526,31 +544,24 @@
 
     hidden = hidden_ref[...]
     hidden_scaled = (hidden.astype(F32) * scale).astype(BF16)
-    def got_2(d, h, k):
-        links.got(along_y(core, lax.rem(y + 4 - d, 4), h), k_p2 + k)
-        links.got(along_x(core, at_x(4 - d), h), k_p2 + 6 + k)
-
-    got_2(3, 0, 0)
-    put_y(lax.rem(y + 1, 4), 0, k_p2 + 4, 3)
-    put_x(at_x(1), 0, k_p2 + 10, 3)
-    to_core(3, 0)
-    for d, h, k in ((1, 0, 2), (1, 1, 3), (3, 1, 1), (2, 1, 5), (2, 0, 4)):
-        got_2(d, h, k)
-        to_core(d, h)
+    got_2(0, 1)
+    got_2(3, 3, relay=True)
+    got_2(1, 3, relay=True)
+    for step, d in ((3, 1), (1, 1), (0, 2), (2, 1), (2, 3), (3, 2), (1, 2), (2, 2)):
+        got_2(step, d)
 
     direct = jnp.zeros((hidden.shape[0], SLOTS), F32)
     down_stores = []
     for turn in range(2):
         k = core if turn == 0 else 1 - core
         if turn == 1:
-            for d in (0, 3, 1, 2):
-                for h in range(2):
-                    from_y, from_x = lax.rem(y + 4 - d, 4), at_x(4 - d)
-                    links.got(along_y(k, from_y, h), k_core + 4 * d + h)
-                    links.got(along_x(k, from_x, h), k_core + 4 * d + 2 + h)
+            for step in range(4):
+                for d in range(4):
+                    for axis in range(2):
+                        links.got(piece(axis, k, step, d), k_core + 16 * axis + 4 * step + d)
         for f in range(4):
             at = pl.ds(pl.multiple_of((2 * f + k) * FSL, FSL), FSL)
-            part = jnp.concatenate([rows[k, (f - n) % 4, n].reshape(2 * HALF, FSL) for n in range(Y)], axis=0)
+            part = jnp.concatenate([rows[k, lax.rem(f - n - 2 * k + 8, 4), n].reshape(2 * HALF, FSL) for n in range(Y)], axis=0)
             direct += nt(w_s[:, at], part)
             down_ref[:, at] = mm(hidden_scaled, part).astype(BF16)
             down_stores.append(load(down_ref.at[:, at], down_hbm.at[:, at], 21 + 4 * turn + f))
@@ -585,7 +596,7 @@
     probg_ref[1:2, :] = jnp.sum(jnp.where(diagonal, out1, 0.0), axis=0, keepdims=True)[:, 0:BLK]
     stores.append(load(probg_ref, probg_hbm, 36))
 
-    @pl.when(t != 0)
+    @pl.when(t != 2 * core)
     def _():
         pltpu.make_async_copy(wmix_ref, wbuf.at[0], local_sems.at[1]).wait()
 
@@ -677,9 +688,11 @@
             pltpu.VMEM((4, 4, 16, FSL), BF16),
             pltpu.VMEM((3, 4, 16, FSL), BF16),
             pltpu.VMEM((4, 16, FSL), BF16),
-            pltpu.VMEM((3, 16, FSL), BF16),
+            pltpu.VMEM((4, 16, FSL), BF16),
             pltpu.VMEM((4, 4, 16, FSL), BF16),
             pltpu.VMEM((4, 4, 16, 128), F32),
+            pltpu.VMEM((16, FSL), BF16),
+            pltpu.VMEM((16, 128), F32),
             pltpu.VMEM((BLK, FSL + 128), F32),
             pltpu.VMEM((BLK, FSL + 128), F32),
             pltpu.VMEM((128, 256), BF16),
@@ -689,7 +702,7 @@
             pltpu.VMEM((hidden, features), BF16),
             pltpu.VMEM((4, 8, 128), F32),
             pltpu.VMEM((4, 8, 128), F32),
-            pltpu.VMEM((4, 8, 128), F32),
+            pltpu.VMEM((5, 8, 128), F32),
             pltpu.VMEM((4, 8, 128), F32),
             pltpu.VMEM((4, 8, 128), F32),
             pltpu.VMEM((NS + BLK, CH), F32),

time: 88.6 us -> 83.6 us (0.944)
  Pallas kernels: 87 us -> 82.8 us
    pallas_call x1, Pallas kernels: 84.3 us -> 80.1 us  [shards(): pl.pallas_call(body, out_shape=(shape((TOK, CH), BF16), shape((TOK, CH),...]
where the time goes in v4:
time: 83.6 us; the launch traced here: 83.4 us
  Pallas kernels  82.8 us (99%)
    pallas_call x1, Pallas kernels, shards(): pl.pallas_call(body, out_shape=(shape((TOK, CH), BF16), shape((TOK, CH),...  80.1 us
    pallas_call x1, Pallas kernels, shards(): pl.pallas_call(store, out_shape=tuple((shape(array.shape, array.dtype) fo...  2.66 us

profile of v4, /device:TPU:1, one launch (start us, length us, event | category | flops | bytes accessed | tf_op | source)
XLA Modules:
  0.0 83.4 jit_solution(8557716240999596805)
XLA Ops:
  0.6 80.1 %scan_and_experts.1 = (bf16[128,128]{1,0:T(8,128)(2,1)}, f32[128,128]{1,0:T(8,128)}, f32[16,128]{1,0:T(8,128)}, f32[16,128]{1,0:T(8,128)}, f32[16,128]{1,0:T(8,1...) custom-call(bf16[128,128]{1,0:T(8,128)(2,1)} %x_hbm.1, ...), custom_call_target="tpu_custom_call" | custom-call | tf_op jit(solution)/shard_map/scan_and_experts/pallas_call | solution.py:633
  80.8 2.7 %store_results.1 = (bf16[128,128]{1,0:T(8,128)(2,1)}, f32[128,128]{1,0:T(8,128)}, f32[16,128]{1,0:T(8,128)}, f32[16,128]{1,0:T(8,128)}, f32[16,128]{1,0:T(8,128)...) custom-call(bf16[128,128]{1,0:T(8,128)(2,1)} %get-tuple-element.27.refs_0_, ...), custom_call_target="tpu_custom_call" | custom-call | tf_op jit(solution)/shard_map/store_results/pallas_call | solution.py:725

commit v5 on v4

--- a/solution.py
+++ b/solution.py
@@ -101,6 +101,24 @@
     def at_z(dz):
         return lax.rem(e + dz, Z)
 
+    def load(src, dst, at):
+        copy = pltpu.make_async_copy(src, dst, local_sems.at[at])
+        copy.start()
+        return copy
+
+    scan_loads = [
+        load(src, dst, 2 + n)
+        for n, (src, dst) in enumerate((
+            (step_hbm, step_ref), (rates_hbm, rates_ref), (x_hbm, x_ref), (g_hbm, g_ref), (inp_hbm, inp_ref),
+            (outp_hbm, outp_ref), (doc_hbm, doc_ref), (skip_hbm, skip_ref), (idx_hbm, idx_ref),
+            (prob_hbm, prob_ref), (resid_hbm, resid_ref),
+        ))
+    ]
+    late_loads = [load(hidden_hbm, hidden_ref, 13)]
+    for n in range(7):
+        part = pl.ds(n * 32, 32)
+        late_loads.append(load(weight_ref.at[part], w_s.at[part], 14 + n))
+
     barrier = pltpu.get_barrier_semaphore()
     partners = 0
     for dc in range(CTX):
@@ -114,23 +132,6 @@
         pl.semaphore_signal(barrier, inc=1, device_id={"exp": at_z(dz)}, device_id_type=MESH)
         partners += 1
 
-    def load(src, dst, at):
-        copy = pltpu.make_async_copy(src, dst, local_sems.at[at])
-        copy.start()
-        return copy
-
-    scan_loads = [
-        load(src, dst, 2 + n)
-        for n, (src, dst) in enumerate((
-            (step_hbm, step_ref), (rates_hbm, rates_ref), (x_hbm, x_ref), (g_hbm, g_ref), (inp_hbm, inp_ref),
-            (outp_hbm, outp_ref), (doc_hbm, doc_ref), (skip_hbm, skip_ref), (idx_hbm, idx_ref),
-            (prob_hbm, prob_ref), (resid_hbm, resid_ref),
-        ))
-    ]
-    late_loads = [load(hidden_hbm, hidden_ref, 13)]
-    for n in range(7):
-        part = pl.ds(n * 32, 32)
-        late_loads.append(load(weight_ref.at[part], w_s.at[part], 14 + n))
     near = (1, 15, 2 + 12 * core)
     for copy in scan_loads:
         copy.wait()
@@ -186,6 +187,14 @@
     xbuf[0, 0:NS] = damp
     xbuf[0, NS : 2 * NS] = state
     xbuf[0, 2 * NS :] = back
+    pl.semaphore_wait(barrier, partners)
+    k_ctx = links.slot(CTX)
+    for dc in range(1, CTX):
+        links.put(xbuf.at[0], xbuf.at[dc], k_ctx + dc, ctx=lax.rem(c + dc, CTX))
+
+    k_pair = links.slot()
+    links.put(pair_out, pair_in, k_pair, ctx=2 * y + (1 - core))
+
     for copy in late_loads:
         copy.wait()
     hidden_t = hidden_ref[...].T
@@ -195,14 +204,25 @@
             for n in range(Y):
                 gs[k, (f - n - 2 * k) % 4, n] = part[n]
 
-    pl.semaphore_wait(barrier, partners)
-    k_ctx = links.slot(CTX)
+    other_core = 2 * y + (1 - core)
+    k_g0 = links.slot(8)
+    for n in range(X):
+        for h in range(2):
+            half = pl.ds(2 * h, 2)
+            links.put(gs.at[1 - core, n, half], g0.at[n, half], k_g0 + 2 * n + h, ctx=other_core)
+
+    links.got(pair_in, k_pair)
+    mine = info
+    theirs = pair_in[:, FSL:]
+    first = core == 0
+    iown[0:BLK] = jnp.where(first, mine, theirs)
+    iown[BLK:] = jnp.where(first, theirs, mine)
+    k_ifar = links.slot(4)
+    for n, dz in enumerate(FAR):
+        links.put(iown, ibuf.at[0, n], k_ifar + n, exp=at_z(dz))
+
     for dc in range(1, CTX):
-        links.put(xbuf.at[0], xbuf.at[dc], k_ctx + dc, ctx=lax.rem(c + dc, CTX))
-
-    k_pair = links.slot()
-    links.put(pair_out, pair_in, k_pair, ctx=2 * y + (1 - core))
-
+        links.got(xbuf.at[dc], k_ctx + dc)
     for turn in range(4):
         dy = lax.rem(t + 2 * core + turn, 4)
         target = {"ctx": at_y(dy), "tp": lax.rem(8 - dy + 2 * core, 4)}
@@ -226,25 +246,6 @@
             copy.start()
             links.started.append(copy)
 
-    other_core = 2 * y + (1 - core)
-    k_g0 = links.slot(8)
-    for n in range(X):
-        for h in range(2):
-            half = pl.ds(2 * h, 2)
-            links.put(gs.at[1 - core, n, half], g0.at[n, half], k_g0 + 2 * n + h, ctx=other_core)
-
-    links.got(pair_in, k_pair)
-    mine = info
-    theirs = pair_in[:, FSL:]
-    first = core == 0
-    iown[0:BLK] = jnp.where(first, mine, theirs)
-    iown[BLK:] = jnp.where(first, theirs, mine)
-    k_ifar = links.slot(4)
-    for n, dz in enumerate(FAR):
-        links.put(iown, ibuf.at[0, n], k_ifar + n, exp=at_z(dz))
-
-    for dc in range(1, CTX):
-        links.got(xbuf.at[dc], k_ctx + dc)
     entering, arriving = zero, zero
     for other in range(CTX):
         from_slot = lax.rem(c - other + CTX, CTX)

time: 83.6 us -> 82.7 us (0.989)
  Pallas kernels: 82.8 us -> 81.9 us
    pallas_call x1, Pallas kernels: 80.1 us -> 79.2 us  [shards(): pl.pallas_call(body, out_shape=(shape((TOK, CH), BF16), shape((TOK, CH),...]
where the time goes in v5:
time: 82.7 us; the launch traced here: 82.6 us
  Pallas kernels  81.9 us (99%)
    pallas_call x1, Pallas kernels, shards(): pl.pallas_call(body, out_shape=(shape((TOK, CH), BF16), shape((TOK, CH),...  79.2 us
    pallas_call x1, Pallas kernels, shards(): pl.pallas_call(store, out_shape=tuple((shape(array.shape, array.dtype) fo...  2.66 us

profile of v5, /device:TPU:1, one launch (start us, length us, event | category | flops | bytes accessed | tf_op | source)
XLA Modules:
  0.0 82.6 jit_solution(17295167774899815960)
XLA Ops:
  0.6 79.2 %scan_and_experts.1 = (bf16[128,128]{1,0:T(8,128)(2,1)}, f32[128,128]{1,0:T(8,128)}, f32[16,128]{1,0:T(8,128)}, f32[16,128]{1,0:T(8,128)}, f32[16,128]{1,0:T(8,1...) custom-call(bf16[128,128]{1,0:T(8,128)(2,1)} %x_hbm.1, ...), custom_call_target="tpu_custom_call" | custom-call | tf_op jit(solution)/shard_map/scan_and_experts/pallas_call | solution.py:634
  79.9 2.7 %store_results.1 = (bf16[128,128]{1,0:T(8,128)(2,1)}, f32[128,128]{1,0:T(8,128)}, f32[16,128]{1,0:T(8,128)}, f32[16,128]{1,0:T(8,128)}, f32[16,128]{1,0:T(8,128)...) custom-call(bf16[128,128]{1,0:T(8,128)(2,1)} %get-tuple-element.27.refs_0_, ...), custom_call_target="tpu_custom_call" | custom-call | tf_op jit(solution)/shard_map/store_results/pallas_call | solution.py:726

commit v6 on v5

--- a/solution.py
+++ b/solution.py
@@ -490,6 +490,8 @@
             pass_on(axis, 0, 0, slot_2(axis, 0, d), d)
     for axis in range(2):
         to_core(axis, 0, 0)
+    got_1(1)
+    got_1(3)
     product = jnp.concatenate(
         [
             picked_rows[0:HALF].astype(F32) * weight_low,
@@ -510,8 +512,6 @@
                     tot_p.at[0], tot_p.at[dk * X + dx], k_tp + dk * X + dx,
                     ctx=2 * y + lax.rem(core + dk, 2), tp=at_x(dx),
                 )
-    got_1(1)
-    got_1(3)
     got_2(0, 3, relay=True)
     got_1(2)
     for n in range(1, 2 * X):

time: 82.7 us -> 83.5 us (level)
  no operation moved by 1% of the time
where the time goes in v6:
time: 83.5 us; the launch traced here: 83.3 us
  Pallas kernels  82.7 us (99%)
    pallas_call x1, Pallas kernels, shards(): pl.pallas_call(body, out_shape=(shape((TOK, CH), BF16), shape((TOK, CH),...  80 us
    pallas_call x1, Pallas kernels, shards(): pl.pallas_call(store, out_shape=tuple((shape(array.shape, array.dtype) fo...  2.66 us

profile of v6, /device:TPU:1, one launch (start us, length us, event | category | flops | bytes accessed | tf_op | source)
XLA Modules:
  0.0 83.3 jit_solution(9682655778645356653)
XLA Ops:
  0.6 80.0 %scan_and_experts.1 = (bf16[128,128]{1,0:T(8,128)(2,1)}, f32[128,128]{1,0:T(8,128)}, f32[16,128]{1,0:T(8,128)}, f32[16,128]{1,0:T(8,128)}, f32[16,128]{1,0:T(8,1...) custom-call(bf16[128,128]{1,0:T(8,128)(2,1)} %x_hbm.1, ...), custom_call_target="tpu_custom_call" | custom-call | tf_op jit(solution)/shard_map/scan_and_experts/pallas_call | solution.py:634
  80.7 2.7 %store_results.1 = (bf16[128,128]{1,0:T(8,128)(2,1)}, f32[128,128]{1,0:T(8,128)}, f32[16,128]{1,0:T(8,128)}, f32[16,128]{1,0:T(8,128)}, f32[16,128]{1,0:T(8,128)...) custom-call(bf16[128,128]{1,0:T(8,128)(2,1)} %get-tuple-element.27.refs_0_, ...), custom_call_target="tpu_custom_call" | custom-call | tf_op jit(solution)/shard_map/store_results/pallas_call | solution.py:726
